TPU v7x, 32 devices: a whole 2x2x4 slice. The times are simulated.
32 devices in a mesh: dp: 16 (over z, y, x), head: 2 (over core).
Axes of the slice: x: 2, y: 2, z: 4, core: 2. Of those that a mesh axis runs over, the one named last changes fastest.
Arguments:
- source_copy: bfloat16 [128, 512, 512], P('dp', 'head'), may hold values from -6 to 6
- target_embed: bfloat16 [128, 512, 512], P('dp', 'head'), may hold values from -6 to 6
- memory: bfloat16 [128, 512, 512], P('dp', 'head'), may hold values from -6 to 6
- tgt_segments: int32 [128, 512], P('dp'), may hold values from 0 to 15, never falling along the last dimension, each value on 1 to 128 neighbouring positions
- src_segments: int32 [128, 512], P('dp'), may hold values from 0 to 15, never falling along the last dimension, each value on 1 to 128 neighbouring positions
- hamming: int32 [128, 16], P('dp'), may hold values from 0 to 64
- priority: int32 [128, 512], P('dp'), may hold values from 0 to 63
- cotangent: bfloat16 [128, 512, 512], P('dp', 'head'), may hold values from -6 to 6
- self_qkv: bfloat16 [3, 512, 512], P(None, None, 'head'), may hold values from -0.25 to 0.25
- self_out: bfloat16 [512, 512], P('head'), may hold values from -1.5 to 1.5
- cross_q: bfloat16 [512, 512], P(None, 'head'), may hold values from -0.25 to 0.25
- cross_kv: bfloat16 [2, 512, 512], P(None, None, 'head'), may hold values from -0.25 to 0.25
- cross_out: bfloat16 [512, 512], P('head'), may hold values from -1.5 to 1.5
- ffn_in: bfloat16 [512, 2048], P(None, 'head'), may hold values from -0.25 to 0.25
- ffn_out: bfloat16 [2048, 512], P('head'), may hold values from -0.125 to 0.125
- head_bias: bfloat16 [4, 512], P(None, 'head'), may hold values from -1.75 to 1.75
- ffn_bias: bfloat16 [2048], P('head'), may hold values from -1.75 to 1.75
- out_bias: bfloat16 [3, 512], replicated, may hold values from -1.75 to 1.75
- norm_gain: bfloat16 [3, 512], replicated, may hold values from 0.5 to 1.5
- norm_shift: bfloat16 [3, 512], replicated, may hold values from -1.75 to 1.75
Outputs:
- first_out: bfloat16 [128, 512, 512], P('dp', 'head')
- second_out: bfloat16 [128, 512, 512], P('dp', 'head')
- input_grad: bfloat16 [128, 512, 512], P('dp', 'head')
- memory_grad: bfloat16 [128, 512, 512], P('dp', 'head')
- self_qkv_grad: float32 [3, 512, 512], P(None, None, 'head')
- self_out_grad: float32 [512, 512], P('head')
- cross_q_grad: float32 [512, 512], P(None, 'head')
- cross_kv_grad: float32 [2, 512, 512], P(None, None, 'head')
- cross_out_grad: float32 [512, 512], P('head')
- ffn_in_grad: float32 [512, 2048], P(None, 'head')
- ffn_out_grad: float32 [2048, 512], P('head')
- head_bias_grad: float32 [4, 512], P(None, 'head')
- ffn_bias_grad: float32 [2048], P('head')
- out_bias_grad: float32 [3, 512], replicated
- gain_grad: float32 [3, 512], replicated
- shift_grad: float32 [3, 512], replicated
Inputs may be any that keep to these rules, and one draw needn't show every extreme that they name: `hamming`: one count for each sentence number of a row; a position is glanced when its priority level is below its sentence's count. A priority level of each target position, drawn independently, ties allowed.
All inputs are finite; a program needn't handle non-finite values.
Results may differ from a plain program's by a relative error of at most 0.034.
Values may be sent and summed in bfloat16 or wider, within the bound.
A program may use at most 256 MiB of HBM per device.

v0:
```python
import jax
import jax.numpy as jnp
from jax import lax
from jax.sharding import PartitionSpec as P

HEAD_DIM = 64


def norm_rows(sums, gain_row, shift_row):
    row_mean = jnp.mean(sums, axis=-1, keepdims=True)
    centred = sums - row_mean
    spread = jnp.mean(centred * centred, axis=-1, keepdims=True)
    return centred * lax.rsqrt(spread + 1e-05) * gain_row + shift_row


def gelu_exact(values):
    return jax.nn.gelu(values, approximate=False)


def project(left, right):
    return jnp.dot(left, right, preferred_element_type=jnp.float32)


def back_project(grads, weight):
    return jnp.einsum("bln,mn->blm", grads, weight, preferred_element_type=jnp.float32)


def weight_grad(left, right):
    return jnp.einsum("blm,bln->mn", left, right, preferred_element_type=jnp.float32)


def row_total(values):
    return jnp.sum(values.astype(jnp.float32), axis=(0, 1))


def masked_scores(block_q, heads_k, block_seg, row_kseg, factor):
    scores = (
        jnp.einsum("qhd,khd->hqk", block_q, heads_k, preferred_element_type=jnp.float32) * factor
    )
    return jnp.where((block_seg[:, None] == row_kseg[None, :])[None], scores, -1e30)


def attend_forward(queries, key_rows, value_rows, query_seg, key_seg, head_dim):
    length = queries.shape[1]
    key_length = key_rows.shape[1]
    local_width = queries.shape[2]
    local_heads = local_width // head_dim
    block_rows = min(512, length)
    blocks = length // block_rows
    factor = head_dim ** (-0.5)

    def one_row(row_items):
        row_q, row_k, row_v, row_qseg, row_kseg = row_items
        heads_k = row_k.reshape(key_length, local_heads, head_dim)
        heads_v = row_v.reshape(key_length, local_heads, head_dim)

        def one_block(block_index):
            block_q = row_q.reshape(block_rows, local_heads, head_dim)
            masked = masked_scores(block_q, heads_k, row_qseg, row_kseg, factor)
            row_peak = jnp.max(masked, axis=-1, keepdims=True)
            log_total = row_peak + jnp.log(
                jnp.sum(jnp.exp(masked - row_peak), axis=-1, keepdims=True)
            )
            probs_low = jnp.exp(masked - log_total).astype(jnp.bfloat16)
            context = jnp.einsum(
                "hqk,khd->qhd", probs_low, heads_v, preferred_element_type=jnp.float32
            )
            return (
                context.reshape(block_rows, local_width).astype(jnp.bfloat16),
                log_total[:, :, 0],
            )

        contexts, log_totals = lax.map(one_block, jnp.arange(blocks))
        return (contexts.reshape(length, local_width), log_totals)

    return lax.map(one_row, (queries, key_rows, value_rows, query_seg, key_seg))


def attend_backward(
    queries, key_rows, value_rows, query_seg, key_seg, log_totals, context_grad, head_dim
):
    length = queries.shape[1]
    key_length = key_rows.shape[1]
    local_width = queries.shape[2]
    local_heads = local_width // head_dim
    block_rows = min(512, length)
    blocks = length // block_rows
    factor = head_dim ** (-0.5)

    def one_row(row_items):
        row_q, row_k, row_v, row_qseg, row_kseg, row_totals, row_grad = row_items
        heads_k = row_k.reshape(key_length, local_heads, head_dim)
        heads_v = row_v.reshape(key_length, local_heads, head_dim)

        def one_block(running, block_index):
            keys_grad, values_grad = running
            block_q = row_q.reshape(block_rows, local_heads, head_dim)
            block_grad = row_grad.reshape(block_rows, local_heads, head_dim)
            masked = masked_scores(block_q, heads_k, row_qseg, row_kseg, factor)
            probs = jnp.exp(masked - row_totals[block_index][:, :, None])
            probs_grad = jnp.einsum(
                "qhd,khd->hqk", block_grad, heads_v, preferred_element_type=jnp.float32
            )
            scores_grad = (
                probs * (probs_grad - jnp.sum(probs_grad * probs, axis=-1, keepdims=True))
            ).astype(jnp.bfloat16)
            query_grad = (
                jnp.einsum("hqk,khd->qhd", scores_grad, heads_k, preferred_element_type=jnp.float32)
                * factor
            )
            keys_grad = (
                keys_grad
                + jnp.einsum(
                    "hqk,qhd->khd", scores_grad, block_q, preferred_element_type=jnp.float32
                )
                * factor
            )
            values_grad = values_grad + jnp.einsum(
                "hqk,qhd->khd",
                probs.astype(jnp.bfloat16),
                block_grad,
                preferred_element_type=jnp.float32,
            )
            return (
                (keys_grad, values_grad),
                query_grad.reshape(block_rows, local_width).astype(jnp.bfloat16),
            )

        empty = jnp.zeros((key_length, local_heads, head_dim), jnp.float32)
        (keys_grad, values_grad), query_blocks = lax.scan(
            one_block, (empty, empty), jnp.arange(blocks)
        )
        return (
            query_blocks.reshape(length, local_width),
            keys_grad.reshape(key_length, local_width),
            values_grad.reshape(key_length, local_width),
        )

    return lax.map(
        one_row, (queries, key_rows, value_rows, query_seg, key_seg, log_totals, context_grad)
    )


def branch_total(partial_value):
    return lax.psum_scatter(
        partial_value.astype(jnp.bfloat16), "head", scatter_dimension=1, tiled=True
    ).astype(jnp.float32)


def gather_share(shares):
    return lax.all_gather(shares, "head", axis=1, tiled=True)


def grad_total(partial_value):
    return lax.psum_scatter(
        partial_value.astype(jnp.bfloat16), "head", scatter_dimension=1, tiled=True
    ).astype(jnp.float32)


def norm_back(sums, gain_row, shift_row, incoming):
    unused, pull = jax.vjp(norm_rows, sums, gain_row, shift_row)
    return pull(incoming)


def glance_mix(tgt_rows, prio_rows, hamming, target_rows, source_rows):
    levels = jnp.arange(hamming.shape[1], dtype=jnp.int32)
    chosen = (tgt_rows[:, :, None] == levels[None, None, :]).astype(jnp.int32)
    limits = jnp.sum(chosen * hamming[:, None, :], axis=2)
    return jnp.where((prio_rows < limits)[:, :, None], target_rows, source_rows)


def body(
    source_copy,
    target_embed,
    memory,
    tgt_segments,
    src_segments,
    hamming,
    priority,
    cotangent,
    self_qkv,
    self_out,
    cross_q,
    cross_kv,
    cross_out,
    ffn_in,
    ffn_out,
    head_bias,
    ffn_bias,
    out_bias,
    norm_gain,
    norm_shift,
):
    head_dim = HEAD_DIM
    share_count = source_copy.shape[1]
    first_share = lax.axis_index("head") * share_count
    gains = norm_gain.astype(jnp.float32)
    shifts = norm_shift.astype(jnp.float32)
    source_full, target_full, memory_full = (
        lax.all_gather(source_copy, "head", axis=1, tiled=True),
        lax.all_gather(target_embed, "head", axis=1, tiled=True),
        lax.all_gather(memory, "head", axis=1, tiled=True),
    )
    mixed_full = glance_mix(tgt_segments, priority, hamming, target_full, source_full)
    cross_keys = project(memory_full, cross_kv[0]).astype(jnp.bfloat16)
    cross_values = (project(memory_full, cross_kv[1]) + head_bias[3]).astype(jnp.bfloat16)

    def forward(inputs_full):
        inputs_share = lax.dynamic_slice_in_dim(inputs_full, first_share, share_count, 1).astype(
            jnp.float32
        )
        queries = (project(inputs_full, self_qkv[0]) + head_bias[0]).astype(jnp.bfloat16)
        key_rows = project(inputs_full, self_qkv[1]).astype(jnp.bfloat16)
        value_rows = (project(inputs_full, self_qkv[2]) + head_bias[1]).astype(jnp.bfloat16)
        context, self_totals = attend_forward(
            queries, key_rows, value_rows, tgt_segments, tgt_segments, head_dim
        )
        first_sum = inputs_share + (branch_total(project(context, self_out)) + out_bias[0])
        first_norm = norm_rows(first_sum, gains[0], shifts[0])
        first_full = gather_share(first_norm.astype(jnp.bfloat16))
        cross_queries = (project(first_full, cross_q) + head_bias[2]).astype(jnp.bfloat16)
        cross_context, cross_totals = attend_forward(
            cross_queries, cross_keys, cross_values, tgt_segments, src_segments, head_dim
        )
        second_sum = first_norm + (branch_total(project(cross_context, cross_out)) + out_bias[1])
        second_norm = norm_rows(second_sum, gains[1], shifts[1])
        second_full = gather_share(second_norm.astype(jnp.bfloat16))
        hidden_pre = project(second_full, ffn_in) + ffn_bias
        hidden = gelu_exact(hidden_pre).astype(jnp.bfloat16)
        third_sum = second_norm + (branch_total(project(hidden, ffn_out)) + out_bias[2])
        output = norm_rows(third_sum, gains[2], shifts[2])
        kept_values = (
            queries,
            key_rows,
            value_rows,
            context,
            self_totals,
            first_sum,
            first_full,
            cross_queries,
            cross_context,
            cross_totals,
            second_sum,
            second_full,
            hidden_pre,
            hidden,
            third_sum,
        )
        return (output, kept_values)

    first_output, unused_kept = forward(source_full)
    second_output, kept_values = forward(mixed_full)
    (
        queries,
        key_rows,
        value_rows,
        context,
        self_totals,
        first_sum,
        first_full,
        cross_queries,
        cross_context,
        cross_totals,
        second_sum,
        second_full,
        hidden_pre,
        hidden,
        third_sum,
    ) = kept_values
    third_grad, gain_two, shift_two = norm_back(
        third_sum, gains[2], shifts[2], cotangent.astype(jnp.float32)
    )
    fed_grad = third_grad.astype(jnp.bfloat16)
    fed_full = gather_share(fed_grad)
    ffn_out_grad = weight_grad(hidden, fed_full)
    hidden_grad = back_project(fed_full, ffn_out).astype(jnp.bfloat16)
    unused_gelu, gelu_pull = jax.vjp(gelu_exact, hidden_pre)
    pre_grad = gelu_pull(hidden_grad.astype(jnp.float32))[0].astype(jnp.bfloat16)
    ffn_in_grad = weight_grad(second_full, pre_grad)
    ffn_bias_grad = row_total(pre_grad)
    second_grad = third_grad + grad_total(back_project(pre_grad, ffn_in))
    second_in, gain_one, shift_one = norm_back(second_sum, gains[1], shifts[1], second_grad)
    crossed_grad = second_in.astype(jnp.bfloat16)
    crossed_full = gather_share(crossed_grad)
    cross_out_grad = weight_grad(cross_context, crossed_full)
    cross_context_grad = back_project(crossed_full, cross_out).astype(jnp.bfloat16)
    cross_query_grad, cross_key_part, cross_value_part = attend_backward(
        cross_queries,
        cross_keys,
        cross_values,
        tgt_segments,
        src_segments,
        cross_totals,
        cross_context_grad,
        head_dim,
    )
    cross_key_grad = cross_key_part.astype(jnp.bfloat16)
    cross_value_grad = cross_value_part.astype(jnp.bfloat16)
    cross_q_grad = weight_grad(first_full, cross_query_grad)
    cross_kv_grad = jnp.stack(
        [weight_grad(memory_full, cross_key_grad), weight_grad(memory_full, cross_value_grad)]
    )
    cross_bias_grad = jnp.stack([row_total(cross_query_grad), row_total(cross_value_grad)])
    memory_part = back_project(cross_key_grad, cross_kv[0]) + back_project(
        cross_value_grad, cross_kv[1]
    )
    memory_grad = lax.psum_scatter(
        memory_part.astype(jnp.bfloat16), "head", scatter_dimension=1, tiled=True
    )
    first_grad = second_in + grad_total(back_project(cross_query_grad, cross_q))
    first_in, gain_zero, shift_zero = norm_back(first_sum, gains[0], shifts[0], first_grad)
    attended_grad = first_in.astype(jnp.bfloat16)
    attended_full = gather_share(attended_grad)
    self_out_grad = weight_grad(context, attended_full)
    context_grad = back_project(attended_full, self_out).astype(jnp.bfloat16)
    query_grad, key_part, value_part = attend_backward(
        queries,
        key_rows,
        value_rows,
        tgt_segments,
        tgt_segments,
        self_totals,
        context_grad,
        head_dim,
    )
    key_grad = key_part.astype(jnp.bfloat16)
    value_grad = value_part.astype(jnp.bfloat16)
    self_qkv_grad = jnp.stack(
        [
            weight_grad(mixed_full, query_grad),
            weight_grad(mixed_full, key_grad),
            weight_grad(mixed_full, value_grad),
        ]
    )
    self_bias_grad = jnp.stack([row_total(query_grad), row_total(value_grad)])
    input_part = (
        back_project(query_grad, self_qkv[0])
        + back_project(key_grad, self_qkv[1])
        + back_project(value_grad, self_qkv[2])
    )
    input_grad = (first_in + grad_total(input_part)).astype(jnp.bfloat16)
    (
        self_qkv_grad,
        self_out_grad,
        self_bias_grad,
        cross_q_grad,
        cross_kv_grad,
        cross_out_grad,
        cross_bias_grad,
        ffn_in_grad,
        ffn_out_grad,
        ffn_bias_grad,
    ) = (
        lax.psum(self_qkv_grad.astype(jnp.bfloat16), "dp").astype(jnp.float32),
        lax.psum(self_out_grad.astype(jnp.bfloat16), "dp").astype(jnp.float32),
        lax.psum(self_bias_grad.astype(jnp.bfloat16), "dp").astype(jnp.float32),
        lax.psum(cross_q_grad.astype(jnp.bfloat16), "dp").astype(jnp.float32),
        lax.psum(cross_kv_grad.astype(jnp.bfloat16), "dp").astype(jnp.float32),
        lax.psum(cross_out_grad.astype(jnp.bfloat16), "dp").astype(jnp.float32),
        lax.psum(cross_bias_grad.astype(jnp.bfloat16), "dp").astype(jnp.float32),
        lax.psum(ffn_in_grad.astype(jnp.bfloat16), "dp").astype(jnp.float32),
        lax.psum(ffn_out_grad.astype(jnp.bfloat16), "dp").astype(jnp.float32),
        lax.psum(ffn_bias_grad.astype(jnp.bfloat16), "dp").astype(jnp.float32),
    )
    head_bias_grad = jnp.concatenate([self_bias_grad, cross_bias_grad], axis=0)
    out_bias_part = jnp.stack(
        [row_total(attended_grad), row_total(crossed_grad), row_total(fed_grad)]
    )
    gain_part = jnp.stack([gain_zero, gain_one, gain_two])
    shift_part = jnp.stack([shift_zero, shift_one, shift_two])
    out_bias_grad, gain_grad, shift_grad = lax.psum(
        (out_bias_part, gain_part, shift_part), ("dp", "head")
    )
    return (
        first_output.astype(jnp.bfloat16),
        second_output.astype(jnp.bfloat16),
        input_grad,
        memory_grad,
        self_qkv_grad,
        self_out_grad,
        cross_q_grad,
        cross_kv_grad,
        cross_out_grad,
        ffn_in_grad,
        ffn_out_grad,
        head_bias_grad,
        ffn_bias_grad,
        out_bias_grad,
        gain_grad,
        shift_grad,
    )


def solution(mesh):
    return jax.shard_map(
        body,
        mesh=mesh,
        in_specs=(
            P("dp", "head", None),
            P("dp", "head", None),
            P("dp", "head", None),
            P("dp", None),
            P("dp", None),
            P("dp", None),
            P("dp", None),
            P("dp", "head", None),
            P(None, None, "head"),
            P("head", None),
            P(None, "head"),
            P(None, None, "head"),
            P("head", None),
            P(None, "head"),
            P("head", None),
            P(None, "head"),
            P("head"),
            P(),
            P(),
            P(),
        ),
        out_specs=(
            P("dp", "head", None),
            P("dp", "head", None),
            P("dp", "head", None),
            P("dp", "head", None),
            P(None, None, "head"),
            P("head", None),
            P(None, "head"),
            P(None, None, "head"),
            P("head", None),
            P(None, "head"),
            P("head", None),
            P(None, "head"),
            P("head"),
            P(),
            P(),
            P(),
        ),
        check_vma=False,
    )
```

profile of v0, /device:TPU:0, one launch (start us, length us, event | category | flops | bytes accessed | tf_op | source)
XLA Modules:
  0.0 1326.4 jit_solution(10038492047703943134)
XLA Ops:
  9.0 17.0 %all-gather.11.cloned.1.call-done = bf16[8,512,512]{2,1,0:T(8,128)(2,1)} async-done(((bf16[8,256,512]{2,1,0:T(8,128)(2,1)}), bf16[8,512,512]{2,1,0:T(8,128)(2,1)}) %all-gather.11.cloned.1.call-update) | async-done | bytes 4194320 | tf_op jit(solution)/shard_map/all_gather | solution.py:200
  26.0 16.4 %all-gather.19.cloned.1.call-done = bf16[8,512,512]{2,1,0:T(8,128)(2,1)} async-done(((bf16[8,256,512]{2,1,0:T(8,128)(2,1)}), bf16[8,512,512]{2,1,0:T(8,128)(2,1)}) %all-gather.19.cloned.1.call-update) | async-done | bytes 4194320 | tf_op jit(solution)/shard_map/all_gather | solution.py:201
  54.4 4.8 add_convert_fusion.5
  59.2 3.9 copy.105
  63.1 3.9 copy.104
  68.6 41.6 %while.71 = (s32[]{:T(128)}, bf16[8,512,256]{1,2,0:T(8,128)(2,1)}, f32[8,1,4,512]{3,2,1,0:T(4,128)S(1)}, s32[8,512]{1,0:T(8,128)S(1)}, bf16[8,512,256]{1,2,0:T(8...) while((s32[]{:T(128)}, bf16[8,512,256]{1,2,0:T(8,128)(2,1)}, ...), condition=%wide.region_21.22_spmd, body=%wide.region_18.21_spmd.sunk | while | flops 280360960 | bytes 16849508 | solution.py:76
  110.2 5.7 convolution_convert_fusion.2
  116.2 4.9 add_convert_fusion.10
  127.9 84.2 %while.69 = (s32[]{:T(128)}, bf16[8,512,256]{1,2,0:T(8,128)(2,1)}, s32[8,512]{1,0:T(8,128)S(1)}, bf16[8,512,256]{2,1,0:T(8,128)(2,1)}, bf16[8,512,256]{1,2,0:T(8...) while((s32[]{:T(128)}, bf16[8,512,256]{1,2,0:T(8,128)(2,1)}, s32[8,512]{1,0:T(8,128)S(1)}, ...), condition=%wide.region_3.4_spmd, body=%wide.region_0.3_spmd.sunk | while | flops 280360960 | bytes 34667124 | solution.py:76
  212.2 4.9 convolution_convert_fusion.4
  220.0 10.4 reduce-scatter.11.cloned.1.call-done
  230.5 5.1 fusion.71
  246.8 4.8 add_convert_fusion.9
  251.6 3.9 copy.99
  255.5 5.4 convolution_convert_fusion.10
  260.9 4.0 copy.101
  265.2 4.8 add_convert_fusion.4
  269.9 4.0 copy.108
  275.4 54.9 %while.72 = (s32[]{:T(128)}, bf16[8,512,256]{1,2,0:T(8,128)(2,1)}, f32[8,1,4,512]{3,2,1,0:T(4,128)S(1)}, bf16[8,512,256]{1,2,0:T(8,128)(2,1)}, s32[8,512]{1,0:T(...) while((s32[]{:T(128)}, bf16[8,512,256]{1,2,0:T(8,128)(2,1)}, ...), condition=%wide.region_28.29_spmd, body=%wide.region_25.28_spmd.sunk | while | flops 280360960 | bytes 16855660 | solution.py:76
  330.3 4.9 convolution_convert_fusion.1
  336.2 4.8 add_convert_fusion.8
  342.4 89.6 %while.70 = (s32[]{:T(128)}, bf16[8,512,256]{1,2,0:T(8,128)(2,1)}, bf16[8,512,256]{1,2,0:T(8,128)(2,1)}, s32[8,512]{1,0:T(8,128)S(1)}, s32[8,512]{1,0:T(8,128)},...) while((s32[]{:T(128)}, bf16[8,512,256]{1,2,0:T(8,128)(2,1)}, ...), condition=%wide.region_10.11_spmd, body=%wide.region_7.10_spmd.sunk | while | flops 280360960 | bytes 18420348 | solution.py:76
  432.1 4.9 convolution_convert_fusion.3
  437.1 13.3 %reduce-scatter.13.cloned.1.call-done = bf16[8,256,512]{2,1,0:T(8,128)(2,1)} async-done(((bf16[8,512,512]{2,1,0:T(8,128)(2,1)}), bf16[8,256,512]{2,1,0:T(8,128)(2,1)}) %reduce-scatter.13.cloned.1.call-update) | async-done | bytes 2097168 | tf_op jit(solution)/shard_map/reduce_scatter | solution.py:145
  450.4 6.5 fusion.191
  464.5 14.1 %all-gather.17.cloned.1.call-done = bf16[8,512,512]{2,1,0:T(8,128)(2,1)} async-done(((bf16[8,256,512]{2,1,0:T(8,128)(2,1)}), bf16[8,512,512]{2,1,0:T(8,128)(2,1)}) %all-gather.17.cloned.1.call-update) | async-done | bytes 4194320 | tf_op jit(solution)/shard_map/all_gather | solution.py:151
  478.6 10.6 fusion.101
  489.2 6.4 all-gather.23.cloned.1.call-done
  495.6 21.3 %fusion.69 = (u8[512,1024]{1,0:T(8,128)(4,1)S(1)}, u8[512,1024]{1,0:T(8,128)(4,1)S(1)}, u8[512,1024]{1,0:T(8,128)(4,1)S(1)}, u8[512,1024]{1,0:T(8,128)(4,1)S(1)}, f32[8,512,1024]{2,1,0:T(8,128)}) fusion(f32[1024]{0:T(1024)S(1)} %convert_element_type.482, f32[8,512,1024]{2,1,0:T(8,128)} %fusion.101, bf16[8,512,512]{2,1,0:T(8,128)(2,1)} %all-gather.23.cloned.1.call-done, ...), kind=kOutput, calls=%fused_computation.213 | convolution fusion | flops 4410310656 | bytes 40898560 | tf_op jit(solution)/shard_map/dot_general | solution.py:21
  516.9 42.5 %fusion.77 = bf16[8,512,512]{2,1,0:T(8,128)(2,1)} fusion(f32[8,512,1024]{2,1,0:T(8,128)} %fusion.101, f32[1024]{0:T(1024)S(1)} %convert_element_type.482, u8[512,1024]{1,0:T(8,128)(4,1)S(1)} %get-tuple-element.641, u8[512,1024]{1,0:T(8,128)(4,1)S(1)} %get-tuple-element.642, bf16[1024,512]{1,0:T(8,128)(2,1)S(1)} %copy-done.100), kind=kOutput, calls=%fused_computation.224 | convolution fusion | flops 4594860032 | bytes 23072768 | tf_op jit(solution)/shard_map/dot_general | solution.py:21
  559.5 40.7 %multiply_convert_fusion.2 = (bf16[8,512,1024]{2,1,0:T(8,128)(2,1)S(1)}, f32[8,512,1024]{2,1,0:T(8,128)}) fusion(f32[8,512,1024]{2,1,0:T(8,128)} %get-tuple-element.833, f32[1024]{0:T(1024)S(1)} %convert_element_type.482, u8[512,1024]{1,0:T(8,128)(4,1)S(1)} %get-tuple-element.629, u8[512,1024]{1,0:T(8,128)(4,1)S(1)} %get-tuple-element.628), kind=kLoop, calls=%fused_computation.135 | loop fusion | flops 297795584 | bytes 42995712 | tf_op jit(solution)/shard_map/convert_element_type | solution.py:229
  603.5 6.1 convolution_convert_fusion.6
  609.7 13.3 %reduce-scatter.21.cloned.1.call-done = bf16[8,256,512]{2,1,0:T(8,128)(2,1)} async-done(((bf16[8,512,512]{2,1,0:T(8,128)(2,1)}), bf16[8,256,512]{2,1,0:T(8,128)(2,1)}) %reduce-scatter.21.cloned.1.call-update) | async-done | bytes 2097168 | tf_op jit(solution)/shard_map/reduce_scatter | solution.py:145
  623.0 6.6 fusion.189
  641.0 15.1 %all-gather.25.cloned.1.call-done = bf16[8,512,512]{2,1,0:T(8,128)(2,1)} async-done(((bf16[8,256,512]{2,1,0:T(8,128)(2,1)}), bf16[8,512,512]{2,1,0:T(8,128)(2,1)}) %all-gather.25.cloned.1.call-update) | async-done | bytes 4194320 | tf_op jit(solution)/shard_map/all_gather | solution.py:151
  656.1 18.8 %fusion.195 = (bf16[1024]{0:T(1024)(128)(2,1)}, bf16[8,512,1024]{2,1,0:T(8,128)(2,1)}) fusion(f32[8,512,1024]{2,1,0:T(8,128)} %get-tuple-element.778, bf16[8,512,512]{2,1,0:T(8,128)(2,1)} %all-gather.25.cloned.1.call-done, bf16[1024,512]{1,0:T(8,128)(2,1)S(1)} %copy-done.101, f32[8,512,1024]{2,1,0:T(8,128)} %get-tuple-element.833, ...), kind=kOutput, calls=%fused_computation.398 | convolution fusion | flops 4370463744 | bytes 47192064 | tf_op jit(solution)/shard_map/bln,mn->blm/dot_general | solution.py:25
  674.9 9.6 convolution_convert_fusion.5
  684.6 13.3 %reduce-scatter.23.cloned.1.call-done = bf16[8,256,512]{2,1,0:T(8,128)(2,1)} async-done(((bf16[8,512,512]{2,1,0:T(8,128)(2,1)}), bf16[8,256,512]{2,1,0:T(8,128)(2,1)}) %reduce-scatter.23.cloned.1.call-update) | async-done | bytes 2097168 | tf_op jit(solution)/shard_map/reduce_scatter | solution.py:155
  697.9 8.7 multiply_reduce_fusion.2
  707.5 6.1 fusion.187
  718.2 14.9 %all-gather.27.cloned.1.call-done = bf16[8,512,512]{2,1,0:T(8,128)(2,1)} async-done(((bf16[8,256,512]{2,1,0:T(8,128)(2,1)}), bf16[8,512,512]{2,1,0:T(8,128)(2,1)}) %all-gather.27.cloned.1.call-update) | async-done | bytes 4194320 | tf_op jit(solution)/shard_map/all_gather | solution.py:151
  733.0 4.8 convolution_convert_fusion.8
  742.4 147.0 %while.73 = (s32[]{:T(128)}, bf16[8,512,256]{1,2,0:T(8,128)(2,1)}, bf16[8,512,256]{1,2,0:T(8,128)(2,1)}, bf16[8,512,256]{1,2,0:T(8,128)(2,1)}, bf16[8,512,256]{1...) while((s32[]{:T(128)}, bf16[8,512,256]{1,2,0:T(8,128)(2,1)}, ...), condition=%wide.region_42.43_spmd, body=%wide.region_40.42_spmd.sunk | while | flops 687601664 | bytes 56169644 | solution.py:139
  806.7 3.9 multiply_reduce_fusion.14
  889.5 5.0 convolution_convert_fusion
  894.6 13.3 %reduce-scatter.25.cloned.1.call-done = bf16[8,256,512]{2,1,0:T(8,128)(2,1)} async-done(((bf16[8,512,512]{2,1,0:T(8,128)(2,1)}), bf16[8,256,512]{2,1,0:T(8,128)(2,1)}) %reduce-scatter.25.cloned.1.call-update) | async-done | bytes 2097168 | tf_op jit(solution)/shard_map/reduce_scatter | solution.py:155
  908.0 4.8 multiply_reduce_fusion.3
  921.4 10.3 bitcast_convert_fusion.1
  931.7 8.9 bitcast_convert_fusion
  951.7 4.8 convolution_convert_fusion.7
  961.0 141.3 %while.74 = (s32[]{:T(128)}, bf16[8,512,256]{1,2,0:T(8,128)(2,1)}, bf16[8,512,256]{1,2,0:T(8,128)(2,1)}, bf16[8,512,256]{1,2,0:T(8,128)(2,1)}, s32[8,512]{1,0:T(...) while((s32[]{:T(128)}, bf16[8,512,256]{1,2,0:T(8,128)(2,1)}, ...), condition=%wide.region_48.49_spmd, body=%wide.region_46.48_spmd.sunk | while | flops 687601664 | bytes 56163488 | solution.py:139
  987.2 3.9 multiply_reduce_fusion.15
  1004.9 3.9 multiply_reduce_fusion.15
  1022.5 3.9 multiply_reduce_fusion.15
  1040.2 3.9 multiply_reduce_fusion.15
  1057.8 3.9 multiply_reduce_fusion.15
  1075.5 3.9 multiply_reduce_fusion.15
  1093.1 3.9 multiply_reduce_fusion.15
  1102.3 4.3 fusion.92
  1135.8 43.2 %all-reduce = (f32[3,512]{1,0:T(4,128)}, f32[3,512]{1,0:T(4,128)}, f32[3,512]{1,0:T(4,128)}) all-reduce(f32[3,512]{1,0:T(4,128)S(1)} %pad_maximum_fusion.2, f32[3,512]{1,0:T(4,128)S(1)} %pad_maximum_fusion.3, f32[3,512]{1,0:T(4,128)S(1)} %pad_maximum_fusion.4), channel_id=1, replica_groups=mesh['dp'=16,'head'=2] {'dp','head'}, use_global_device_ids=true, to_apply=%region_69.70 | all-reduce | flops 4608 | bytes 36864 | tf_op jit(solution)/shard_map/psum | solution.py:371
  1181.4 40.4 %all-reduce.1 = (bf16[2,256]{1,0:T(2,128)(2,1)S(1)}, bf16[2,256]{1,0:T(2,128)(2,1)S(1)}, bf16[1024]{0:T(1024)(128)(2,1)S(1)}) all-reduce(bf16[2,256]{1,0:T(2,128)(2,1)S(1)} %pad_maximum_fusion.6, bf16[2,256]{1,0:T(2,128)(2,1)S(1)} %pad_maximum_fusion.5, bf16[1024]{0:T(1024)(128)(2,1)S(1)} %copy-done.94), channel_id=1, replica_groups=mesh['dp'=16,'head'=2] {'dp'}, use_global_device_ids=true, to_apply=%region_63.64 | all-reduce | flops 2048 | bytes 8192 | tf_op jit(solution)/shard_map/psum | solution.py:360
  1222.9 67.0 %all-reduce.5.cloned.1.call-done = (bf16[2,512,256]{1,2,0:T(8,128)(2,1)}, bf16[3,512,256]{2,1,0:T(8,128)(2,1)}, bf16[256,512]{1,0:T(8,128)(2,1)}, bf16[512,256]{...) async-done(((bf16[2,512,256]{1,2,0:T(8,128)(2,1)}, bf16[3,512,256]{2,1,0:T(8,128)(2,1)}, ...) | async-done | bytes 4194320 | tf_op jit(solution)/shard_map/psum | solution.py:358
  1303.1 4.7 add_convert_fusion.2
  1307.8 11.6 reduce-scatter.29.cloned.1.call-done
  (968 shorter events, 668.3 us)
Async XLA Ops:
  7.2 471.4 %copy-start = (bf16[512,1024]{1,0:T(8,128)(2,1)S(1)}, bf16[512,1024]{1,0:T(8,128)(2,1)}, u32[]{:S(2)}) copy-start(bf16[512,1024]{1,0:T(8,128)(2,1)} %param.45) | copy-start | bytes 3145732
  7.2 18.8 %all-gather.11.cloned.1.call-start = ((), (), s32[]{:S(2)}) async-start(), calls=%async_computation.10 | async-start | bytes 6291456 | tf_op jit(solution)/shard_map/all_gather | solution.py:200
  8.0 34.5 %all-gather.19.cloned.1.call-start = ((), (), s32[]{:S(2)}) async-start(), calls=%async_computation.17 | async-start | bytes 6291456 | tf_op jit(solution)/shard_map/all_gather | solution.py:201
  8.7 211.3 %reduce-scatter.17.cloned.1.call-start = ((), (), s32[]{:S(2)}) async-start(), calls=%async_computation.18 | async-start | bytes 6291456 | tf_op jit(solution)/shard_map/reduce_scatter | solution.py:145
  9.0 37.3 %copy-start.34 = (bf16[3,512,256]{2,1,0:T(8,128)(2,1)S(1)}, bf16[3,512,256]{2,1,0:T(8,128)(2,1)}, u32[]{:S(2)}) copy-start(bf16[3,512,256]{2,1,0:T(8,128)(2,1)} %param.40) | copy-start | bytes 2359300
  68.6 41.6 %copy-start.39 = (bf16[256,512]{1,0:T(8,128)(2,1)S(1)}, bf16[256,512]{1,0:T(8,128)(2,1)}, u32[]{:S(2)}) copy-start(bf16[256,512]{1,0:T(8,128)(2,1)} %param.41) | copy-start | bytes 786436
  115.9 114.6 %reduce-scatter.11.cloned.1.call-start = ((), (), s32[]{:S(2)}) async-start(), calls=%async_computation.11 | async-start | bytes 6291456 | tf_op jit(solution)/shard_map/reduce_scatter | solution.py:145
  217.1 29.8 %all-gather.13.cloned.1.call-start = ((), (), s32[]{:S(2)}) async-start(), calls=%async_computation.12 | async-start | bytes 6291456 | tf_op jit(solution)/shard_map/all_gather | solution.py:202
  217.7 47.5 %all-gather.21.cloned.1.call-start = ((), (), s32[]{:S(2)}) async-start(), calls=%async_computation.19 | async-start | bytes 6291456 | tf_op jit(solution)/shard_map/all_gather | solution.py:151
  218.8 231.6 %copy-start.66 = (f32[1,512]{1,0:T(1,128)}, f32[1,512]{1,0:T(1,128)S(1)}, u32[]{:S(2)}) copy-start(f32[1,512]{1,0:T(1,128)S(1)} %get-tuple-element.818) | copy-start | bytes 6148
  219.4 231.0 %copy-start.72 = (f32[1,512]{1,0:T(1,128)}, f32[1,512]{1,0:T(1,128)S(1)}, u32[]{:S(2)}) copy-start(f32[1,512]{1,0:T(1,128)S(1)} %get-tuple-element.823) | copy-start | bytes 6148
  219.4 240.4 %copy-start.74 = (f32[1,512]{1,0:T(1,128)}, f32[1,512]{1,0:T(1,128)S(1)}, u32[]{:S(2)}) copy-start(f32[1,512]{1,0:T(1,128)S(1)} %get-tuple-element.822) | copy-start | bytes 6148
  220.0 239.8 %copy-start.76 = (f32[1,512]{1,0:T(1,128)}, f32[1,512]{1,0:T(1,128)S(1)}, u32[]{:S(2)}) copy-start(f32[1,512]{1,0:T(1,128)S(1)} %get-tuple-element.825) | copy-start | bytes 6148
  230.5 5.9 copy-start.21
  235.5 214.9 %copy-start.46 = (f32[8,256]{1,0:T(8,128)}, f32[8,256]{1,0:T(8,128)S(1)}, u32[]{:S(2)}) copy-start(f32[8,256]{1,0:T(8,128)S(1)} %get-tuple-element.836) | copy-start | bytes 24580
  239.9 210.5 %copy-start.58 = (f32[8,256]{1,0:T(8,128)}, f32[8,256]{1,0:T(8,128)S(1)}, u32[]{:S(2)}) copy-start(f32[8,256]{1,0:T(8,128)S(1)} %fusion.145) | copy-start | bytes 24580
  243.8 91.7 %all-gather.15.cloned.1.call-start = ((), (), s32[]{:S(2)}) async-start(), calls=%async_computation.13 | async-start | bytes 6291456 | tf_op jit(solution)/shard_map/all_gather | solution.py:151
  264.9 172.2 %reduce-scatter.19.cloned.1.call-start = ((), (), s32[]{:S(2)}) async-start(), calls=%async_computation.20 | async-start | bytes 6291456 | tf_op jit(solution)/shard_map/reduce_scatter | solution.py:145
  275.4 54.9 %copy-start.37 = (bf16[256,512]{1,0:T(8,128)(2,1)S(1)}, bf16[256,512]{1,0:T(8,128)(2,1)}, u32[]{:S(2)}) copy-start(bf16[256,512]{1,0:T(8,128)(2,1)} %param.44) | copy-start | bytes 786436
  335.3 115.1 %reduce-scatter.13.cloned.1.call-start = ((), (), s32[]{:S(2)}) async-start(), calls=%async_computation.14 | async-start | bytes 6291456 | tf_op jit(solution)/shard_map/reduce_scatter | solution.py:145
  437.0 41.6 %all-gather.17.cloned.1.call-start = ((), (), s32[]{:S(2)}) async-start(), calls=%async_computation.15 | async-start | bytes 6291456 | tf_op jit(solution)/shard_map/all_gather | solution.py:151
  463.5 32.1 %all-gather.23.cloned.1.call-start = ((), (), s32[]{:S(2)}) async-start(), calls=%async_computation.21 | async-start | bytes 6291456 | tf_op jit(solution)/shard_map/all_gather | solution.py:151
  464.2 145.5 %reduce-scatter.15.cloned.1.call-start = ((), (), s32[]{:S(2)}) async-start(), calls=%async_computation.16 | async-start | bytes 6291456 | tf_op jit(solution)/shard_map/reduce_scatter | solution.py:145
  489.2 27.7 %copy-start.100 = (bf16[1024,512]{1,0:T(8,128)(2,1)S(1)}, bf16[1024,512]{1,0:T(8,128)(2,1)}, u32[]{:S(2)}) copy-start(bf16[1024,512]{1,0:T(8,128)(2,1)} %param.46) | copy-start | bytes 3145732
  559.4 63.5 %reduce-scatter.21.cloned.1.call-start = ((), (), s32[]{:S(2)}) async-start(), calls=%async_computation.22 | async-start | bytes 6291456 | tf_op jit(solution)/shard_map/reduce_scatter | solution.py:145
  609.5 13.4 %copy-start.49 = (f32[8,256]{1,0:T(8,128)S(1)}, f32[8,256]{1,0:T(8,128)}, u32[]{:S(2)}) copy-start(f32[8,256]{1,0:T(8,128)} %copy-done.48) | copy-start | bytes 24580
  609.5 13.4 %copy-start.51 = (f32[8,256]{1,0:T(8,128)S(1)}, f32[8,256]{1,0:T(8,128)}, u32[]{:S(2)}) copy-start(f32[8,256]{1,0:T(8,128)} %copy-done.50) | copy-start | bytes 24580
  609.5 13.4 %copy-start.61 = (f32[8,256]{1,0:T(8,128)S(1)}, f32[8,256]{1,0:T(8,128)}, u32[]{:S(2)}) copy-start(f32[8,256]{1,0:T(8,128)} %copy-done.60) | copy-start | bytes 24580
  609.5 13.4 %copy-start.63 = (f32[8,256]{1,0:T(8,128)S(1)}, f32[8,256]{1,0:T(8,128)}, u32[]{:S(2)}) copy-start(f32[8,256]{1,0:T(8,128)} %copy-done.62) | copy-start | bytes 24580
  609.5 13.4 %copy-start.75 = (f32[1,512]{1,0:T(1,128)S(1)}, f32[1,512]{1,0:T(1,128)}, u32[]{:S(2)}) copy-start(f32[1,512]{1,0:T(1,128)} %copy-done.74) | copy-start | bytes 6148
  609.5 13.4 %copy-start.77 = (f32[1,512]{1,0:T(1,128)S(1)}, f32[1,512]{1,0:T(1,128)}, u32[]{:S(2)}) copy-start(f32[1,512]{1,0:T(1,128)} %copy-done.76) | copy-start | bytes 6148
  609.6 13.4 %copy-start.79 = (f32[1,512]{1,0:T(1,128)S(1)}, f32[1,512]{1,0:T(1,128)}, u32[]{:S(2)}) copy-start(f32[1,512]{1,0:T(1,128)} %get-tuple-element.817) | copy-start | bytes 6148
  609.6 46.5 %all-gather.25.cloned.1.call-start = ((), (), s32[]{:S(2)}) async-start(), calls=%async_computation.23 | async-start | bytes 6291456 | tf_op jit(solution)/shard_map/all_gather | solution.py:151
  638.6 17.5 %copy-start.101 = (bf16[1024,512]{1,0:T(8,128)(2,1)S(1)}, bf16[1024,512]{1,0:T(8,128)(2,1)}, u32[]{:S(2)}) copy-start(bf16[1024,512]{1,0:T(8,128)(2,1)} %param.46) | copy-start | bytes 3145732
  641.0 56.9 %reduce-scatter.23.cloned.1.call-start = ((), (), s32[]{:S(2)}) async-start(), calls=%async_computation.24 | async-start | bytes 6291456 | tf_op jit(solution)/shard_map/reduce_scatter | solution.py:155
  684.5 13.4 %copy-start.25 = (bf16[8,256,512]{2,1,0:T(8,128)(2,1)S(1)}, bf16[8,256,512]{2,1,0:T(8,128)(2,1)}, u32[]{:S(2)}) copy-start(bf16[8,256,512]{2,1,0:T(8,128)(2,1)} %reduce-scatter.15.cloned.1.call-done) | copy-start | bytes 6291460
  684.5 48.5 %all-gather.27.cloned.1.call-start = ((), (), s32[]{:S(2)}) async-start(), calls=%async_computation.25 | async-start | bytes 6291456 | tf_op jit(solution)/shard_map/all_gather | solution.py:151
  684.6 22.1 %copy-start.71 = (f32[8,256]{1,0:T(8,128)S(1)}, f32[8,256]{1,0:T(8,128)}, u32[]{:S(2)}) copy-start(f32[8,256]{1,0:T(8,128)} %copy-done.70) | copy-start | bytes 24580
  697.9 8.8 copy-start.5
  697.9 8.8 copy-start.7
  697.9 9.0 copy-start.19
  697.9 9.6 copy-start.32
  715.5 17.5 %copy-start.38 = (bf16[256,512]{1,0:T(8,128)(2,1)S(1)}, bf16[256,512]{1,0:T(8,128)(2,1)}, u32[]{:S(2)}) copy-start(bf16[256,512]{1,0:T(8,128)(2,1)} %param.44) | copy-start | bytes 786436
  717.9 190.0 %reduce-scatter.25.cloned.1.call-start = ((), (), s32[]{:S(2)}) async-start(), calls=%async_computation.26 | async-start | bytes 6291456 | tf_op jit(solution)/shard_map/reduce_scatter | solution.py:155
  742.4 147.0 %copy-start.54 = (bf16[512,256]{1,0:T(8,128)(2,1)S(1)}, bf16[512,256]{1,0:T(8,128)(2,1)}, u32[]{:S(2)}) copy-start(bf16[512,256]{1,0:T(8,128)(2,1)} %param.42) | copy-start | bytes 786436
  889.5 18.5 %copy-start.9 = (bf16[8,256,512]{2,1,0:T(8,128)(2,1)S(1)}, bf16[8,256,512]{2,1,0:T(8,128)(2,1)}, u32[]{:S(2)}) copy-start(bf16[8,256,512]{2,1,0:T(8,128)(2,1)} %reduce-scatter.17.cloned.1.call-done) | copy-start | bytes 6291460
  889.5 18.5 %copy-start.47 = (f32[8,256]{1,0:T(8,128)S(1)}, f32[8,256]{1,0:T(8,128)}, u32[]{:S(2)}) copy-start(f32[8,256]{1,0:T(8,128)} %copy-done.46) | copy-start | bytes 24580
  889.5 18.5 %copy-start.59 = (f32[8,256]{1,0:T(8,128)S(1)}, f32[8,256]{1,0:T(8,128)}, u32[]{:S(2)}) copy-start(f32[8,256]{1,0:T(8,128)} %copy-done.58) | copy-start | bytes 24580
  889.5 18.5 %copy-start.67 = (f32[1,512]{1,0:T(1,128)S(1)}, f32[1,512]{1,0:T(1,128)}, u32[]{:S(2)}) copy-start(f32[1,512]{1,0:T(1,128)} %copy-done.66) | copy-start | bytes 6148
  889.5 18.5 %copy-start.73 = (f32[1,512]{1,0:T(1,128)S(1)}, f32[1,512]{1,0:T(1,128)}, u32[]{:S(2)}) copy-start(f32[1,512]{1,0:T(1,128)} %copy-done.72) | copy-start | bytes 6148
  894.6 18.2 %copy-start.69 = (f32[8,256]{1,0:T(8,128)S(1)}, f32[8,256]{1,0:T(8,128)}, u32[]{:S(2)}) copy-start(f32[8,256]{1,0:T(8,128)} %copy-done.68) | copy-start | bytes 24580
  894.6 57.1 %all-gather.29.cloned.1.call-start = ((), (), s32[]{:S(2)}) async-start(), calls=%async_computation.27 | async-start | bytes 6291456 | tf_op jit(solution)/shard_map/all_gather | solution.py:151
  908.0 5.9 copy-start.17
  908.0 6.5 copy-start.27
  920.9 369.0 %all-reduce.5.cloned.1.call-start = ((), (), s32[]{:S(2)}) async-start(), calls=%async_computation.30 | async-start | bytes 8388608 | tf_op jit(solution)/shard_map/psum | solution.py:358
  921.4 10.3 copy-start.97
  931.7 8.9 copy-start.23
  931.7 8.9 copy-start.95
  1115.9 187.2 %reduce-scatter.27.cloned.1.call-start = ((), (), s32[]{:S(2)}) async-start(), calls=%async_computation.28 | async-start | bytes 6291456 | tf_op jit(solution)/shard_map/reduce_scatter | solution.py:155
  1125.1 194.2 %reduce-scatter.29.cloned.1.call-start = ((), (), s32[]{:S(2)}) async-start(), calls=%async_computation.29 | async-start | bytes 6291456 | tf_op jit(solution)/shard_map/reduce_scatter | solution.py:307
  1131.7 49.7 %copy-start.94 = (bf16[1024]{0:T(1024)(128)(2,1)S(1)}, bf16[1024]{0:T(1024)(128)(2,1)}, u32[]{:S(2)}) copy-start(bf16[1024]{0:T(1024)(128)(2,1)} %get-tuple-element.834) | copy-start | bytes 6148
  1289.9 7.1 copy-start.43
  1292.8 6.2 copy-start.56
  1292.8 7.1 copy-start.55
  (87 other events, 288.4 us)
Sparse Core Ops, SparseCore 0:
  9.6 16.3 all-gather.10
  27.6 14.8 all-gather.18
  116.0 13.2 reduce-scatter.16
  217.2 13.2 reduce-scatter.10
  231.9 14.9 all-gather.12
  248.8 14.8 all-gather.20
  265.8 14.8 all-gather.14
  335.4 13.2 reduce-scatter.18
  437.1 13.2 reduce-scatter.12
  463.6 14.9 all-gather.16
  480.7 14.8 all-gather.22
  559.5 13.2 reduce-scatter.14
  609.7 13.1 reduce-scatter.20
  641.1 14.9 all-gather.24
  684.6 13.2 reduce-scatter.22
  718.0 14.9 all-gather.26
  894.7 13.1 reduce-scatter.24
  921.1 14.9 all-gather.28
  1116.0 173.8 all-reduce.4
  1292.1 10.8 reduce-scatter.26
  1305.9 13.3 reduce-scatter.28
where the time goes:
time: 1340 us; the launch traced here: 1330 us
  matrix products  481 us (36%)
  local copies, waits for them, and re-layouts  312 us (23%)
  waiting for transfers between devices  234 us (17%)
  other arithmetic  194 us (14%)
  blocking collectives  83.6 us (6%)
  between operations  15.7 us (1%)
    dynamic_slice x224, local copies, waits for them, and re-layouts, attend_forward(): return lax.map(one_row, (queries, key_rows, value_rows, query_seg, key_seg))  180 us
    dot_general x18, matrix products, project(): return jnp.dot(left, right, preferred_element_type=jnp.float32)  141 us
    dot_general x48, matrix products, masked_scores(): jnp.einsum('qhd,khd->hqk', block_q, heads_k, preferred_element_type=jnp.f...  81.9 us
    psum x1, waiting for transfers between devices, body(): lax.psum(cross_kv_grad.astype(jnp.bfloat16), 'dp').astype(jnp.float32)  67 us
    dot_general x16, matrix products, one_block(): jnp.einsum('qhd,khd->hqk', block_grad, heads_v, preferred_element_type=jn...  61.7 us
    dot_general x10, matrix products, back_project(): jnp.einsum('bln,mn->blm', grads, weight, preferred_element_type=jnp.float32)  58.2 us
    dot_general x32, matrix products, one_block(): jnp.einsum('hqk,khd->qhd', probs_low, heads_v, preferred_element_type=jnp...  57.6 us
    all_gather x7, waiting for transfers between devices, gather_share(): return lax.all_gather(shares, 'head', axis=1, tiled=True)  50.5 us
  transfers between devices with their start and end apart: 21, of which 15 were waited for; matrix products, arithmetic and copies ran while one was open for 31% of the time, Pallas kernels for 0%

commit v1 on v0

v1 whole, which is shorter than its diff:
```python
import functools

import jax
import jax.numpy as jnp
import numpy as np
from jax import lax
from jax.experimental import pallas as pl
from jax.experimental.pallas import tpu as pltpu
from jax.sharding import PartitionSpec as P

HEAD_DIM = 64
PAIR = 2 * HEAD_DIM
TILE = 128
WINDOW = 256
FAR = -1e30
F32 = jnp.float32
BF16 = jnp.bfloat16
VMEM_BYTES = 60 * 1024 * 1024


def dot_nn(left, right):
    return lax.dot_general(left, right, (((1,), (0,)), ((), ())), preferred_element_type=F32)


def dot_nt(left, right):
    return lax.dot_general(left, right, (((1,), (1,)), ((), ())), preferred_element_type=F32)


def norm_stats(sums):
    row_mean = jnp.mean(sums, axis=-1, keepdims=True)
    centred = sums - row_mean
    spread = jnp.mean(centred * centred, axis=-1, keepdims=True)
    inverse = lax.rsqrt(spread + 1e-05)
    return centred * inverse, inverse


def norm_back(sums, gain_row, incoming):
    normed, inverse = norm_stats(sums)
    scaled = incoming * gain_row
    mean_one = jnp.mean(scaled, axis=-1, keepdims=True)
    mean_two = jnp.mean(scaled * normed, axis=-1, keepdims=True)
    grad = (scaled - mean_one - normed * mean_two) * inverse
    gain_part = jnp.sum(incoming * normed, axis=0, keepdims=True)
    shift_part = jnp.sum(incoming, axis=0, keepdims=True)
    return grad, gain_part, shift_part


def gelu_parts(pre):
    size = jnp.abs(pre) * 0.7071067811865476
    ratio = 1.0 / (1.0 + 0.3275911 * size)
    series = ratio * (
        0.254829592
        + ratio
        * (-0.284496736 + ratio * (1.421413741 + ratio * (-1.453152027 + ratio * 1.061405429)))
    )
    bell = jnp.exp(-(size * size))
    tail = 0.5 * series * bell
    phi = jnp.where(pre >= 0, 1.0 - tail, tail)
    return phi, bell * 0.3989422804014327


def each_tile(count, step):
    def one(index, carry):
        step(index)
        return carry

    lax.fori_loop(0, count, one, 0)


def window_loop(starts_ref, base, tiles, length, step):
    def one(tile):
        start = starts_ref[base + tile]

        @pl.when(start >= 0)
        def near():
            step(tile, pl.multiple_of(start, 16), min(WINDOW, length))

        if length > WINDOW:

            @pl.when(start < 0)
            def whole():
                step(tile, 0, length)

    each_tile(tiles, one)


def attend(q_ref, k_ref, v_ref, far_ref, near_ref, sides_ref, ctx_ref, lse_ref, starts_ref, base):
    length, width = q_ref.shape
    pairs = width // PAIR
    left, right = sides_ref[0], sides_ref[1]

    def step(tile, start, window):
        rows = pl.ds(pl.multiple_of(tile * TILE, TILE), TILE)
        keys = pl.ds(start, window)
        query_marks = far_ref[rows, :]
        key_marks = near_ref[keys, :]
        for pair in range(pairs):
            lanes = slice(pair * PAIR, (pair + 1) * PAIR)
            queries = q_ref[rows, lanes]
            stacked = jnp.concatenate(
                [
                    jnp.concatenate([queries * left, query_marks], axis=1),
                    jnp.concatenate([queries * right, query_marks], axis=1),
                ],
                axis=0,
            )
            key_side = jnp.concatenate([k_ref[keys, lanes], key_marks], axis=1)
            scores = dot_nt(key_side, stacked)
            peak = jnp.max(scores, axis=0, keepdims=True)
            weights = jnp.exp(scores - peak)
            total = jnp.sum(weights, axis=0, keepdims=True)
            mixed = dot_nn(v_ref[keys, lanes].T, weights.astype(BF16))
            share = 1.0 / total
            context = jnp.concatenate(
                [
                    mixed[:HEAD_DIM, :TILE] * share[:, :TILE],
                    mixed[HEAD_DIM:, TILE:] * share[:, TILE:],
                ],
                axis=0,
            )
            ctx_ref[rows, lanes] = context.T.astype(BF16)
            if lse_ref is not None:
                log_total = peak + jnp.log(total)
                lse_ref[tile, pl.ds(2 * pair, 1), :] = log_total[:, :TILE]
                lse_ref[tile, pl.ds(2 * pair + 1, 1), :] = log_total[:, TILE:]

    window_loop(starts_ref, base, length // TILE, length, step)


def three_parts(values):
    high = values.astype(BF16).astype(F32)
    rest = values - high
    middle = rest.astype(BF16).astype(F32)
    return high, middle, rest - middle


def attend_back(
    q_ref,
    k_ref,
    v_ref,
    far_ref,
    near_ref,
    sides_ref,
    own_ref,
    spread_ref,
    lse_ref,
    ctx_ref,
    dctx_ref,
    dq_ref,
    dk_ref,
    dv_ref,
    starts_ref,
    base,
):
    length, width = q_ref.shape
    pairs = width // PAIR
    heads = width // HEAD_DIM
    left, right = sides_ref[0], sides_ref[1]
    dk_ref[...] = jnp.zeros_like(dk_ref)
    dv_ref[...] = jnp.zeros_like(dv_ref)

    def step(tile, start, window):
        rows = pl.ds(pl.multiple_of(tile * TILE, TILE), TILE)
        keys = pl.ds(start, window)
        key_marks = near_ref[keys, :]
        high, middle, low = three_parts(-lse_ref[tile])
        stats = jnp.concatenate(
            [
                jnp.zeros((16, TILE), F32),
                high,
                middle,
                low,
                jnp.zeros((TILE - 16 - 3 * heads, TILE), F32),
            ],
            axis=0,
        )
        query_marks = far_ref[rows, :] + stats.T.astype(BF16)
        product = dctx_ref[rows, :].astype(F32) * ctx_ref[rows, :].astype(F32)
        product_high = product.astype(BF16)
        product_low = (product - product_high.astype(F32)).astype(BF16)
        delta = -(dot_nn(product_high, spread_ref[...]) + dot_nn(product_low, spread_ref[...]))
        high, middle, low = three_parts(delta)
        lane = lax.broadcasted_iota(jnp.int32, delta.shape, 1)
        grad_marks = jnp.where(
            lane < 16 + heads, high, jnp.where(lane < 16 + 2 * heads, middle, low)
        ).astype(BF16)
        for pair in range(pairs):
            lanes = slice(pair * PAIR, (pair + 1) * PAIR)
            queries = q_ref[rows, lanes]
            grads = dctx_ref[rows, lanes]
            key_rows = k_ref[keys, lanes]
            query_stack = jnp.concatenate([queries * left, queries * right], axis=0)
            grad_stack = jnp.concatenate([grads * left, grads * right], axis=0)
            own = (own_ref[2 * pair], own_ref[2 * pair + 1])
            query_side = jnp.concatenate(
                [
                    query_stack,
                    jnp.concatenate([query_marks * own[0], query_marks * own[1]], axis=0),
                ],
                axis=1,
            )
            grad_side = jnp.concatenate(
                [
                    grad_stack,
                    jnp.concatenate([grad_marks * own[0], grad_marks * own[1]], axis=0),
                ],
                axis=1,
            )
            probs = jnp.exp(dot_nt(jnp.concatenate([key_rows, key_marks], axis=1), query_side))
            probs_grad = dot_nt(
                jnp.concatenate([v_ref[keys, lanes], key_marks], axis=1), grad_side
            )
            scores_grad = (probs * probs_grad).astype(BF16)
            dk_ref[keys, lanes] += dot_nn(scores_grad, query_stack)
            dv_ref[keys, lanes] += dot_nn(probs.astype(BF16), grad_stack)
            turned = dot_nn(key_rows.T, scores_grad)
            turned = jnp.concatenate(
                [turned[:HEAD_DIM, :TILE], turned[HEAD_DIM:, TILE:]], axis=0
            )
            dq_ref[rows, lanes] = (turned.T * (HEAD_DIM**-0.5)).astype(BF16)

    window_loop(starts_ref, base, length // TILE, length, step)


def attention_kernel(
    starts_ref,
    x_ref,
    memory_ref,
    far_ref,
    near_self_ref,
    near_cross_ref,
    sides_ref,
    self_qkv_ref,
    self_out_ref,
    cross_q_ref,
    cross_kv_ref,
    cross_out_ref,
    head_bias_ref,
    out_bias_ref,
    gain_ref,
    shift_ref,
    q_ref,
    k_ref,
    v_ref,
    ctx_ref,
    lse_ref,
    r1_ref,
    a1_ref,
    q2_ref,
    k2_ref,
    v2_ref,
    ctx2_ref,
    lse2_ref,
    r2_ref,
    work_ref,
):
    row = pl.program_id(0)
    tiles = x_ref.shape[0] // TILE
    self_part(
        starts_ref,
        row,
        x_ref,
        far_ref,
        near_self_ref,
        sides_ref,
        self_qkv_ref,
        self_out_ref,
        head_bias_ref,
        out_bias_ref,
        gain_ref,
        shift_ref,
        q_ref,
        k_ref,
        v_ref,
        ctx_ref,
        lse_ref,
        r1_ref,
        a1_ref,
        work_ref,
    )
    k2_ref[...] = dot_nn(memory_ref[...], cross_kv_ref[0]).astype(BF16)
    v2_ref[...] = (dot_nn(memory_ref[...], cross_kv_ref[1]) + head_bias_ref[3:4, :]).astype(BF16)
    cross_part(
        starts_ref,
        pl.num_programs(0) * tiles + row * tiles,
        far_ref,
        near_cross_ref,
        sides_ref,
        cross_q_ref,
        cross_out_ref,
        head_bias_ref,
        out_bias_ref,
        a1_ref,
        q2_ref,
        k2_ref,
        v2_ref,
        ctx2_ref,
        lse2_ref,
        r2_ref,
        work_ref,
    )


def self_part(
    starts_ref,
    row,
    x_ref,
    far_ref,
    near_ref,
    sides_ref,
    self_qkv_ref,
    self_out_ref,
    head_bias_ref,
    out_bias_ref,
    gain_ref,
    shift_ref,
    q_ref,
    k_ref,
    v_ref,
    ctx_ref,
    lse_ref,
    r1_ref,
    a1_ref,
    work_ref,
):
    tiles = x_ref.shape[0] // TILE
    inputs = x_ref[...]
    queries = (dot_nn(inputs, self_qkv_ref[0]) + head_bias_ref[0:1, :]).astype(BF16)
    q_ref[...] = queries * jnp.asarray(HEAD_DIM**-0.5, BF16)
    k_ref[...] = dot_nn(inputs, self_qkv_ref[1]).astype(BF16)
    v_ref[...] = (dot_nn(inputs, self_qkv_ref[2]) + head_bias_ref[1:2, :]).astype(BF16)
    attend(
        q_ref, k_ref, v_ref, far_ref, near_ref, sides_ref, ctx_ref, lse_ref, starts_ref, row * tiles
    )
    work_ref[...] = dot_nn(ctx_ref[...], self_out_ref[...])

    def step(tile):
        rows = pl.ds(pl.multiple_of(tile * TILE, TILE), TILE)
        sums = x_ref[rows, :].astype(F32) + (work_ref[rows, :] + out_bias_ref[0:1, :])
        if r1_ref is not None:
            r1_ref[rows, :] = sums
        normed = norm_stats(sums)[0] * gain_ref[0:1, :] + shift_ref[0:1, :]
        work_ref[rows, :] = normed
        a1_ref[rows, :] = normed.astype(BF16)

    each_tile(tiles, step)


def cross_part(
    starts_ref,
    base,
    far_ref,
    near_ref,
    sides_ref,
    cross_q_ref,
    cross_out_ref,
    head_bias_ref,
    out_bias_ref,
    a1_ref,
    q2_ref,
    k2_ref,
    v2_ref,
    ctx2_ref,
    lse2_ref,
    r2_ref,
    work_ref,
):
    queries = (dot_nn(a1_ref[...], cross_q_ref[...]) + head_bias_ref[2:3, :]).astype(BF16)
    q2_ref[...] = queries * jnp.asarray(HEAD_DIM**-0.5, BF16)
    attend(
        q2_ref, k2_ref, v2_ref, far_ref, near_ref, sides_ref, ctx2_ref, lse2_ref, starts_ref, base
    )
    r2_ref[...] = work_ref[...] + (
        dot_nn(ctx2_ref[...], cross_out_ref[...]) + out_bias_ref[1:2, :]
    )


def feed_part(r2_ref, a2_ref, work_ref, ffn_in_ref, ffn_out_ref, ffn_bias_ref, gain_ref, shift_ref, keep):
    length = r2_ref.shape[0]
    hidden = ffn_in_ref.shape[1]

    def step(tile):
        rows = pl.ds(pl.multiple_of(tile * TILE, TILE), TILE)
        normed = norm_stats(r2_ref[rows, :])[0] * gain_ref[1:2, :] + shift_ref[1:2, :]
        work_ref[rows, :] = normed
        a2_ref[rows, :] = normed.astype(BF16)

    each_tile(length // TILE, step)
    chunk = 256
    for first in range(0, hidden, chunk):
        units = slice(first, first + chunk)
        pre = dot_nn(a2_ref[...], ffn_in_ref[:, units]) + ffn_bias_ref[:, units]
        phi, bell = gelu_parts(pre)
        active = (pre * phi).astype(BF16)
        if keep is not None:
            keep[0][:, units] = active
            keep[1][:, units] = (phi + pre * bell).astype(BF16)
        work_ref[...] += dot_nn(active, ffn_out_ref[units, :])


def feed_kernel(
    r2_ref,
    cot_ref,
    ffn_in_ref,
    ffn_out_ref,
    ffn_bias_ref,
    out_bias_ref,
    gain_ref,
    shift_ref,
    out_ref,
    a2_ref,
    g_ref,
    df_ref,
    du_ref,
    dr2_ref,
    do2_ref,
    small_ref,
    ffn_bias_grad_ref,
    slope_ref,
    work_ref,
):
    length = r2_ref.shape[0]
    hidden = ffn_in_ref.shape[1]
    feed_part(
        r2_ref,
        a2_ref,
        work_ref,
        ffn_in_ref,
        ffn_out_ref,
        ffn_bias_ref,
        gain_ref,
        shift_ref,
        (g_ref, slope_ref),
    )
    small_ref[...] = jnp.zeros_like(small_ref)

    def last_norm(tile):
        rows = pl.ds(pl.multiple_of(tile * TILE, TILE), TILE)
        sums = work_ref[rows, :] + out_bias_ref[2:3, :]
        normed, inverse = norm_stats(sums)
        out_ref[rows, :] = (normed * gain_ref[2:3, :] + shift_ref[2:3, :]).astype(BF16)
        grad, gain_part, shift_part = norm_back(
            sums, gain_ref[2:3, :], cot_ref[rows, :].astype(F32)
        )
        work_ref[rows, :] = grad
        low = grad.astype(BF16)
        df_ref[rows, :] = low
        small_ref[0:1, :] += gain_part
        small_ref[1:2, :] += shift_part
        small_ref[2:3, :] += jnp.sum(low.astype(F32), axis=0, keepdims=True)

    each_tile(length // TILE, last_norm)
    chunk = 256
    for first in range(0, hidden, chunk):
        units = slice(first, first + chunk)
        hidden_grad = dot_nt(df_ref[...], ffn_out_ref[units, :]).astype(BF16).astype(F32)
        pre_grad = (hidden_grad * slope_ref[:, units].astype(F32)).astype(BF16)
        du_ref[:, units] = pre_grad
        ffn_bias_grad_ref[0:1, units] = jnp.sum(pre_grad.astype(F32), axis=0, keepdims=True)
        work_ref[...] += dot_nt(pre_grad, ffn_in_ref[:, units])

    def middle_norm(tile):
        rows = pl.ds(pl.multiple_of(tile * TILE, TILE), TILE)
        grad, gain_part, shift_part = norm_back(
            r2_ref[rows, :], gain_ref[1:2, :], work_ref[rows, :]
        )
        dr2_ref[rows, :] = grad
        low = grad.astype(BF16)
        do2_ref[rows, :] = low
        small_ref[3:4, :] += gain_part
        small_ref[4:5, :] += shift_part
        small_ref[5:6, :] += jnp.sum(low.astype(F32), axis=0, keepdims=True)

    each_tile(length // TILE, middle_norm)


def cross_back_kernel(
    starts_ref,
    dr2_ref,
    do2_ref,
    q2_ref,
    k2_ref,
    v2_ref,
    ctx2_ref,
    lse2_ref,
    r1_ref,
    far_ref,
    near_ref,
    sides_ref,
    own_ref,
    spread_ref,
    cross_q_ref,
    cross_kv_ref,
    cross_out_ref,
    gain_ref,
    dq_ref,
    dk_low_ref,
    dv_low_ref,
    memory_grad_ref,
    dr1_ref,
    do_ref,
    small_ref,
    dctx_ref,
    dk_ref,
    dv_ref,
    work_ref,
):
    tiles = dr2_ref.shape[0] // TILE
    base = pl.num_programs(0) * tiles + pl.program_id(0) * tiles
    dctx_ref[...] = dot_nt(do2_ref[...], cross_out_ref[...]).astype(BF16)
    attend_back(
        q2_ref,
        k2_ref,
        v2_ref,
        far_ref,
        near_ref,
        sides_ref,
        own_ref,
        spread_ref,
        lse2_ref,
        ctx2_ref,
        dctx_ref,
        dq_ref,
        dk_ref,
        dv_ref,
        starts_ref,
        base,
    )
    dk_low_ref[...] = dk_ref[...].astype(BF16)
    dv_low_ref[...] = dv_ref[...].astype(BF16)
    memory_grad_ref[...] = (
        dot_nt(dk_low_ref[...], cross_kv_ref[0]) + dot_nt(dv_low_ref[...], cross_kv_ref[1])
    ).astype(BF16)
    work_ref[...] = dr2_ref[...] + dot_nt(dq_ref[...], cross_q_ref[...])
    small_ref[...] = jnp.zeros_like(small_ref)

    def first_norm(tile):
        rows = pl.ds(pl.multiple_of(tile * TILE, TILE), TILE)
        grad, gain_part, shift_part = norm_back(
            r1_ref[rows, :], gain_ref[0:1, :], work_ref[rows, :]
        )
        dr1_ref[rows, :] = grad
        low = grad.astype(BF16)
        do_ref[rows, :] = low
        small_ref[0:1, :] += gain_part
        small_ref[1:2, :] += shift_part
        small_ref[2:3, :] += jnp.sum(low.astype(F32), axis=0, keepdims=True)
        small_ref[3:4, :] += jnp.sum(dq_ref[rows, :].astype(F32), axis=0, keepdims=True)
        small_ref[4:5, :] += jnp.sum(dv_low_ref[rows, :].astype(F32), axis=0, keepdims=True)

    each_tile(tiles, first_norm)


def self_back_kernel(
    starts_ref,
    dr1_ref,
    do_ref,
    q_ref,
    k_ref,
    v_ref,
    ctx_ref,
    lse_ref,
    far_ref,
    near_ref,
    sides_ref,
    own_ref,
    spread_ref,
    self_qkv_ref,
    self_out_ref,
    dq_ref,
    dk_low_ref,
    dv_low_ref,
    input_grad_ref,
    small_ref,
    dctx_ref,
    dk_ref,
    dv_ref,
):
    tiles = dr1_ref.shape[0] // TILE
    dctx_ref[...] = dot_nt(do_ref[...], self_out_ref[...]).astype(BF16)
    attend_back(
        q_ref,
        k_ref,
        v_ref,
        far_ref,
        near_ref,
        sides_ref,
        own_ref,
        spread_ref,
        lse_ref,
        ctx_ref,
        dctx_ref,
        dq_ref,
        dk_ref,
        dv_ref,
        starts_ref,
        pl.program_id(0) * tiles,
    )
    dk_low_ref[...] = dk_ref[...].astype(BF16)
    dv_low_ref[...] = dv_ref[...].astype(BF16)
    input_grad_ref[...] = (
        dr1_ref[...]
        + (dot_nt(dq_ref[...], self_qkv_ref[0]) + dot_nt(dk_low_ref[...], self_qkv_ref[1]))
        + dot_nt(dv_low_ref[...], self_qkv_ref[2])
    ).astype(BF16)
    small_ref[...] = jnp.zeros_like(small_ref)

    def totals(tile):
        rows = pl.ds(pl.multiple_of(tile * TILE, TILE), TILE)
        small_ref[0:1, :] += jnp.sum(dq_ref[rows, :].astype(F32), axis=0, keepdims=True)
        small_ref[1:2, :] += jnp.sum(dv_low_ref[rows, :].astype(F32), axis=0, keepdims=True)

    each_tile(tiles, totals)


def first_pass_kernel(
    starts_ref,
    x_ref,
    k2_ref,
    v2_ref,
    far_ref,
    near_self_ref,
    near_cross_ref,
    sides_ref,
    self_qkv_ref,
    self_out_ref,
    cross_q_ref,
    cross_out_ref,
    ffn_in_ref,
    ffn_out_ref,
    head_bias_ref,
    ffn_bias_ref,
    out_bias_ref,
    gain_ref,
    shift_ref,
    out_ref,
    q_ref,
    k_ref,
    v_ref,
    ctx_ref,
    low_ref,
    r2_ref,
    work_ref,
):
    row = pl.program_id(0)
    tiles = x_ref.shape[0] // TILE
    self_part(
        starts_ref,
        row,
        x_ref,
        far_ref,
        near_self_ref,
        sides_ref,
        self_qkv_ref,
        self_out_ref,
        head_bias_ref,
        out_bias_ref,
        gain_ref,
        shift_ref,
        q_ref,
        k_ref,
        v_ref,
        ctx_ref,
        None,
        None,
        low_ref,
        work_ref,
    )
    cross_part(
        starts_ref,
        pl.num_programs(0) * tiles + row * tiles,
        far_ref,
        near_cross_ref,
        sides_ref,
        cross_q_ref,
        cross_out_ref,
        head_bias_ref,
        out_bias_ref,
        low_ref,
        q_ref,
        k2_ref,
        v2_ref,
        ctx_ref,
        None,
        r2_ref,
        work_ref,
    )
    feed_part(
        r2_ref,
        low_ref,
        work_ref,
        ffn_in_ref,
        ffn_out_ref,
        ffn_bias_ref,
        gain_ref,
        shift_ref,
        None,
    )

    def last_norm(tile):
        rows = pl.ds(pl.multiple_of(tile * TILE, TILE), TILE)
        sums = work_ref[rows, :] + out_bias_ref[2:3, :]
        out_ref[rows, :] = (
            norm_stats(sums)[0] * gain_ref[2:3, :] + shift_ref[2:3, :]
        ).astype(BF16)

    each_tile(tiles, last_norm)


def per_row(array):
    block = (None,) + array.shape[1:]
    zeros = (0,) * (len(array.shape) - 1)
    return pl.BlockSpec(block, lambda row, *_: (row,) + zeros)


def whole(array):
    zeros = (0,) * len(array.shape)
    return pl.BlockSpec(array.shape, lambda row, *_: zeros, pipeline_mode=pl.Buffered(1))


def call_rows(kernel, name, rows, scalars, row_args, fixed_args, outs, scratch, flops, order=None):
    args = tuple(row_args) + tuple(fixed_args)
    specs = [per_row(a) for a in row_args] + [whole(a) for a in fixed_args]
    if order is not None:
        args = tuple(args[i] for i in order)
        specs = [specs[i] for i in order]
    out_shapes = tuple(jax.ShapeDtypeStruct(shape, kind) for shape, kind in outs)
    moved = sum(a.size * a.dtype.itemsize for a in args)
    moved += sum(int(np.prod(s.shape)) * s.dtype.itemsize for s in out_shapes)
    return pl.pallas_call(
        kernel,
        grid_spec=pltpu.PrefetchScalarGridSpec(
            num_scalar_prefetch=len(scalars),
            grid=(rows,),
            in_specs=specs,
            out_specs=tuple(per_row(s) for s in out_shapes),
            scratch_shapes=[pltpu.VMEM(shape, kind) for shape, kind in scratch],
        ),
        out_shape=out_shapes,
        compiler_params=pltpu.CompilerParams(
            dimension_semantics=("arbitrary",), vmem_limit_bytes=VMEM_BYTES
        ),
        cost_estimate=pl.CostEstimate(flops=flops, bytes_accessed=moved, transcendentals=0),
        name=name,
    )(*scalars, *args)


def shifted(values, axis, size, step):
    return lax.ppermute(values, axis, [(i, (i + step) % size) for i in range(size)])


def by_origin(parts, me):
    count = len(parts)
    if count == 1:
        return parts
    if count == 2:
        return [
            jnp.where(me == 0, parts[0], parts[1]),
            jnp.where(me == 0, parts[1], parts[0]),
        ]
    stacked = jnp.stack(parts)
    return [
        lax.dynamic_index_in_dim(stacked, (me - origin) % count, 0, keepdims=False)
        for origin in range(count)
    ]


def gather_parts(values, axis, me, size):
    parts = [values] + [shifted(values, "head", size, step) for step in range(1, size)]
    return jnp.concatenate(by_origin(parts, me), axis=axis)


def trade_parts(values, split_axis, join_axis, me, size):
    share = values.shape[split_axis] // size
    parts = []
    for step in range(size):
        target = (me + step) % size
        part = lax.dynamic_slice_in_dim(values, target * share, share, split_axis)
        parts.append(part if step == 0 else shifted(part, "head", size, step))
    return jnp.concatenate(by_origin(parts, me), axis=join_axis)


def head_share(values, axis, me, size):
    share = values.shape[axis] // size
    total = None
    for step in range(size):
        target = (me + step) % size
        part = lax.dynamic_slice_in_dim(values, target * share, share, axis)
        if step > 0:
            part = shifted(part, "head", size, step)
        total = part.astype(F32) if total is None else total + part.astype(F32)
    return total.astype(BF16)


def dp_stages(dp_size, swapped):
    bits = dp_size.bit_length() - 1
    first = [(1 << b, 2) for b in range(min(2, bits))]
    if swapped:
        first = first[::-1]
    if bits > 2:
        first.append((4, 1 << (bits - 2)))
    return first


def dp_permute(values, dp_size, stride, count, step):
    def place(i):
        digit = (i // stride) % count
        return i + (((digit ^ step) - digit) * stride)

    return lax.ppermute(values, "dp", [(i, place(i)) for i in range(dp_size)])


def dp_total(values, dp_size, spot, swapped):
    stages = dp_stages(dp_size, swapped)
    for stride, count in stages:
        digit = (spot // stride) % count
        share = values.shape[0] // count
        total = lax.dynamic_slice_in_dim(values, digit * share, share, 0).astype(F32)
        for step in range(1, count):
            part = lax.dynamic_slice_in_dim(values, (digit ^ step) * share, share, 0)
            total = total + dp_permute(part, dp_size, stride, count, step).astype(F32)
        values = total.astype(BF16)
    for stride, count in stages[::-1]:
        digit = (spot // stride) % count
        share = values.shape[0]
        grown = jnp.zeros((share * count,) + values.shape[1:], values.dtype)
        grown = lax.dynamic_update_slice_in_dim(grown, values, digit * share, 0)
        for step in range(1, count):
            part = dp_permute(values, dp_size, stride, count, step)
            grown = lax.dynamic_update_slice_in_dim(grown, part, (digit ^ step) * share, 0)
        values = grown
    return values


def small_total(values, dp_size, head_size):
    stride = 1
    while stride < dp_size:
        values = values + dp_permute(values, dp_size, stride, 2, 1)
        stride *= 2
    total = values
    for step in range(1, head_size):
        total = total + shifted(values, "head", head_size, step)
    return total


def window_starts(query_segments, key_segments, window):
    rows, length = query_segments.shape
    tiles = query_segments.reshape(rows, length // TILE, TILE)
    first, last = tiles[:, :, 0], tiles[:, :, -1]
    before = jnp.sum(key_segments[:, None, :] < first[:, :, None], axis=2).astype(jnp.int32)
    after = jnp.sum(key_segments[:, None, :] <= last[:, :, None], axis=2).astype(jnp.int32)
    start = jnp.minimum((before // 16) * 16, key_segments.shape[1] - window)
    return jnp.where(after - start <= window, start, -1).reshape(-1)


def token_grad(left, right):
    return lax.dot_general(
        left, right, (((0, 1), (0, 1)), ((), ())), preferred_element_type=F32
    ).astype(BF16)


def constants(width, levels):
    heads = width // HEAD_DIM
    lane = np.arange(PAIR)
    sides = np.stack([lane < HEAD_DIM, lane >= HEAD_DIM])
    own = np.stack(
        [(lane < levels) | ((lane >= 16) & (lane < 16 + 3 * heads) & ((lane - 16) % heads == h)) for h in range(heads)]
    )
    feature = np.arange(width)
    spread = (
        (lane[None, :] >= 16)
        & (lane[None, :] < 16 + 3 * heads)
        & ((lane[None, :] - 16) % heads == feature[:, None] // HEAD_DIM)
    )
    widen = lambda a: np.broadcast_to(a[:, None, :], (a.shape[0], TILE, PAIR))
    ones = (lane >= 16) & (lane < 16 + 3 * heads)
    return (
        jnp.asarray(widen(sides), BF16),
        jnp.asarray(widen(own), BF16),
        jnp.asarray(spread, BF16),
        jnp.asarray(ones, BF16),
    )


def segment_marks(segments, levels, ones):
    lane = jnp.arange(PAIR, dtype=jnp.int32)
    same = segments[:, :, None] == lane[None, None, :]
    far = jnp.where(same | (lane >= levels)[None, None, :], 0.0, FAR).astype(BF16)
    near = jnp.where(same, 1.0, 0.0).astype(BF16)
    return far, near + ones[None, None, :]


def local_layer(source, mixed, memory, cotangent, tgt_segments, src_segments, levels, weights):
    (
        self_qkv,
        self_out,
        cross_q,
        cross_kv,
        cross_out,
        ffn_in,
        ffn_out,
        head_bias,
        ffn_bias,
        out_bias,
        gain,
        shift,
    ) = weights
    rows, length, width = mixed.shape
    hidden = ffn_in.shape[1]
    heads = width // HEAD_DIM
    tiles = length // TILE
    window = min(WINDOW, length)
    sides, own, spread, ones = constants(width, levels)
    far, near_self = segment_marks(tgt_segments, levels, ones)
    near_cross = segment_marks(src_segments, levels, ones)[1]
    starts = jnp.concatenate(
        [
            window_starts(tgt_segments, tgt_segments, window),
            window_starts(tgt_segments, src_segments, window),
        ]
    )
    wide_low = ((rows, length, width), BF16)
    wide = ((rows, length, width), F32)
    stats = ((rows, tiles, heads, TILE), F32)
    small = ((rows, 8, width), F32)
    square = 2 * rows * length * width * width
    scores = 2 * rows * length * window * width
    one_low = ((length, width), BF16)
    one = ((length, width), F32)
    (
        queries,
        key_rows,
        value_rows,
        context,
        totals,
        first_sum,
        first_low,
        cross_queries,
        cross_keys,
        cross_values,
        cross_context,
        cross_totals,
        second_sum,
    ) = call_rows(
        attention_kernel,
        "attention",
        rows,
        (starts,),
        (mixed, memory, far, near_self, near_cross),
        (
            sides,
            self_qkv,
            self_out,
            cross_q,
            cross_kv,
            cross_out,
            head_bias,
            out_bias,
            gain,
            shift,
        ),
        (
            wide_low,
            wide_low,
            wide_low,
            wide_low,
            stats,
            wide,
            wide_low,
            wide_low,
            wide_low,
            wide_low,
            wide_low,
            stats,
            wide,
        ),
        (one,),
        8 * square + 8 * scores,
    )
    (
        second_out,
        second_low,
        hidden_rows,
        fed_grad,
        pre_grad,
        second_in,
        crossed_grad,
        feed_small,
        ffn_bias_part,
    ) = call_rows(
        feed_kernel,
        "feed",
        rows,
        (),
        (second_sum, cotangent),
        (ffn_in, ffn_out, ffn_bias, out_bias, gain, shift),
        (
            wide_low,
            wide_low,
            ((rows, length, hidden), BF16),
            wide_low,
            ((rows, length, hidden), BF16),
            wide,
            wide_low,
            small,
            ((rows, 8, hidden), F32),
        ),
        (((length, hidden), BF16), one),
        4 * square * hidden // width,
    )
    ffn_in_grad = token_grad(second_low, pre_grad)
    ffn_out_grad = token_grad(hidden_rows, fed_grad)
    (
        cross_query_grad,
        cross_key_grad,
        cross_value_grad,
        memory_grad,
        first_in,
        attended_grad,
        cross_small,
    ) = call_rows(
        cross_back_kernel,
        "cross_back",
        rows,
        (starts,),
        (
            second_in,
            crossed_grad,
            cross_queries,
            cross_keys,
            cross_values,
            cross_context,
            cross_totals,
            first_sum,
            far,
            near_cross,
        ),
        (sides, own, spread, cross_q, cross_kv, cross_out, gain),
        (wide_low, wide_low, wide_low, wide_low, wide, wide_low, small),
        (one_low, one, one, one),
        4 * square + 10 * scores,
    )
    cross_q_grad = token_grad(first_low, cross_query_grad)
    cross_k_grad = token_grad(memory, cross_key_grad)
    cross_v_grad = token_grad(memory, cross_value_grad)
    cross_out_grad = token_grad(cross_context, crossed_grad)
    query_grad, key_grad, value_grad, input_grad, self_small = call_rows(
        self_back_kernel,
        "self_back",
        rows,
        (starts,),
        (
            first_in,
            attended_grad,
            queries,
            key_rows,
            value_rows,
            context,
            totals,
            far,
            near_self,
        ),
        (sides, own, spread, self_qkv, self_out),
        (wide_low, wide_low, wide_low, wide_low, small),
        (one_low, one, one),
        4 * square + 10 * scores,
    )
    q_grad = token_grad(mixed, query_grad)
    k_grad = token_grad(mixed, key_grad)
    v_grad = token_grad(mixed, value_grad)
    self_out_grad = token_grad(context, attended_grad)
    source, input_grad = lax.optimization_barrier((source, input_grad))
    (first_out,) = call_rows(
        first_pass_kernel,
        "first_pass",
        rows,
        (starts,),
        (source, cross_keys, cross_values, far, near_self, near_cross),
        (
            sides,
            self_qkv,
            self_out,
            cross_q,
            cross_out,
            ffn_in,
            ffn_out,
            head_bias,
            ffn_bias,
            out_bias,
            gain,
            shift,
        ),
        (wide_low,),
        (one_low, one_low, one_low, one_low, one_low, one, one),
        6 * square + 2 * square * hidden // width + 8 * scores,
    )
    feed_sums = jnp.sum(feed_small, axis=0)
    cross_sums = jnp.sum(cross_small, axis=0)
    self_sums = jnp.sum(self_small, axis=0)
    bias_sums = jnp.sum(ffn_bias_part[:, 0, :], axis=0).reshape(hidden // width, width)
    small_sums = jnp.concatenate(
        [
            self_sums[0:2],
            cross_sums[3:5],
            cross_sums[2:3],
            feed_sums[5:6],
            feed_sums[2:3],
            cross_sums[0:1],
            feed_sums[3:4],
            feed_sums[0:1],
            cross_sums[1:2],
            feed_sums[4:5],
            feed_sums[1:2],
            bias_sums,
        ],
        axis=0,
    )
    return (
        first_out,
        second_out,
        input_grad,
        memory_grad,
        (ffn_in_grad, ffn_out_grad),
        (cross_q_grad, cross_k_grad, cross_v_grad, cross_out_grad),
        (q_grad, k_grad, v_grad, self_out_grad),
        small_sums,
    )


def body(
    dp_size,
    head_size,
    source_copy,
    target_embed,
    memory,
    tgt_segments,
    src_segments,
    hamming,
    priority,
    cotangent,
    self_qkv,
    self_out,
    cross_q,
    cross_kv,
    cross_out,
    ffn_in,
    ffn_out,
    head_bias,
    ffn_bias,
    out_bias,
    norm_gain,
    norm_shift,
):
    me = lax.axis_index("head")
    spot = lax.axis_index("dp")
    levels = hamming.shape[1]
    held, share, width = source_copy.shape
    rows = held // head_size

    def own_positions(array):
        return lax.dynamic_slice_in_dim(array, me * share, share, 1)

    def own_rows(array):
        return lax.dynamic_slice_in_dim(array, me * rows, rows, 0)

    level = jnp.arange(levels, dtype=jnp.int32)
    chosen = own_positions(tgt_segments)[:, :, None] == level[None, None, :]
    limits = jnp.sum(jnp.where(chosen, hamming[:, None, :], 0), axis=2)
    glanced = own_positions(priority) < limits
    mixed_part = jnp.where(glanced[:, :, None], target_embed, source_copy)

    gather = functools.partial(gather_parts, me=me, size=head_size)
    trade = functools.partial(trade_parts, me=me, size=head_size)
    mixed = trade(mixed_part, 0, 1)
    self_qkv = gather(self_qkv, 2)
    self_out = gather(self_out, 0)
    memory_rows = trade(memory, 0, 1)
    cross_q = gather(cross_q, 1)
    cross_kv = gather(cross_kv, 2)
    cross_out = gather(cross_out, 0)
    head_bias = gather(head_bias, 1).astype(F32)
    ffn_bias = gather(ffn_bias[None, :], 1).astype(F32)
    ffn_in = gather(ffn_in, 1)
    ffn_out = gather(ffn_out, 0)
    cot_rows = trade(cotangent, 0, 1)
    source = trade(source_copy, 0, 1)
    (
        first_out,
        second_out,
        input_grad,
        memory_grad,
        feed_grads,
        cross_grads,
        self_grads,
        small_sums,
    ) = local_layer(
        source,
        mixed,
        memory_rows,
        cot_rows,
        own_rows(tgt_segments),
        own_rows(src_segments),
        levels,
        (
            self_qkv,
            self_out,
            cross_q,
            cross_kv,
            cross_out,
            ffn_in,
            ffn_out,
            head_bias,
            ffn_bias,
            out_bias.astype(F32),
            norm_gain.astype(F32),
            norm_shift.astype(F32),
        ),
    )

    def total(values, axis, swapped):
        return dp_total(head_share(values, axis, me, head_size), dp_size, spot, swapped).astype(F32)

    ffn_in_grad = total(feed_grads[0], 1, False)
    ffn_out_grad = total(feed_grads[1], 0, True)
    cross_q_grad = total(cross_grads[0], 1, False)
    cross_kv_grad = jnp.stack([total(cross_grads[1], 1, False), total(cross_grads[2], 1, True)])
    cross_out_grad = total(cross_grads[3], 0, True)
    self_qkv_grad = jnp.stack(
        [
            total(self_grads[0], 1, False),
            total(self_grads[1], 1, True),
            total(self_grads[2], 1, False),
        ]
    )
    self_out_grad = total(self_grads[3], 0, True)
    sums = small_total(small_sums, dp_size, head_size)
    part = width // head_size
    head_bias_grad = lax.dynamic_slice_in_dim(sums[0:4], me * part, part, 1)
    hidden = ffn_in.shape[1] // head_size
    ffn_bias_grad = lax.dynamic_slice_in_dim(sums[13:].reshape(-1), me * hidden, hidden, 0)

    def back(array):
        return trade(array, 1, 0)

    return (
        back(first_out),
        back(second_out),
        back(input_grad),
        back(memory_grad),
        self_qkv_grad,
        self_out_grad,
        cross_q_grad,
        cross_kv_grad,
        cross_out_grad,
        ffn_in_grad,
        ffn_out_grad,
        head_bias_grad,
        ffn_bias_grad,
        sums[4:7],
        sums[7:10],
        sums[10:13],
    )


def solution(mesh):
    return jax.shard_map(
        functools.partial(body, mesh.shape["dp"], mesh.shape["head"]),
        mesh=mesh,
        in_specs=(
            P("dp", "head", None),
            P("dp", "head", None),
            P("dp", "head", None),
            P("dp", None),
            P("dp", None),
            P("dp", None),
            P("dp", None),
            P("dp", "head", None),
            P(None, None, "head"),
            P("head", None),
            P(None, "head"),
            P(None, None, "head"),
            P("head", None),
            P(None, "head"),
            P("head", None),
            P(None, "head"),
            P("head"),
            P(),
            P(),
            P(),
        ),
        out_specs=(
            P("dp", "head", None),
            P("dp", "head", None),
            P("dp", "head", None),
            P("dp", "head", None),
            P(None, None, "head"),
            P("head", None),
            P(None, "head"),
            P(None, None, "head"),
            P("head", None),
            P(None, "head"),
            P("head", None),
            P(None, "head"),
            P("head"),
            P(),
            P(),
            P(),
        ),
        check_vma=False,
    )
```

time: 1340 us -> 681 us (0.51)
  matrix products: 481 us -> 34.2 us
  local copies, waits for them, and re-layouts: 312 us -> 25 us
  Pallas kernels: 0 us -> 278 us
  starting transfers between devices: 3.14 us -> 147 us
  other arithmetic: 194 us -> 55.8 us
  waiting for transfers between devices: 234 us -> 128 us
  blocking collectives: 83.6 us -> 0 us
    dot_general x182 -> x10, matrix products: 481 us -> 34.2 us  [token_grad(): lax.dot_general(left, right, (((0, 1), (0, 1)), ((), ())), preferred_elem...]
    pallas_call x0 -> x5, Pallas kernels: none -> 278 us  [call_rows(): pl.pallas_call(kernel, grid_spec=pltpu.PrefetchScalarGridSpec(num_scalar_...]
    dynamic_slice x224 -> x53, local copies, waits for them, and re-layouts: 180 us -> 14.7 us  [the longest x8 9.03 us: trade_parts(): part = lax.dynamic_slice_in_dim(values, target * share, share, split_axis)]
    ppermute x0 -> x132, starting transfers between devices: none -> 147 us  [the longest x104 137 us: dp_permute(): return lax.ppermute(values, 'dp', [(i, place(i)) for i in range(dp_size)])]
    ppermute x0 -> x132, waiting for transfers between devices: none -> 128 us  [the longest x104 126 us: dp_permute(): return lax.ppermute(values, 'dp', [(i, place(i)) for i in range(dp_size)])]
    reduce_sum x53 -> x6, other arithmetic: 93.7 us -> 3.91 us  [the longest x1 0.98 us: local_layer(): jnp.sum(ffn_bias_part[:, 0, :], axis=0).reshape(hidden // width, width)]
    all_gather x10 -> x0, waiting for transfers between devices: 86.9 us -> none  [the longest x7 50.5 us: gather_share(): return lax.all_gather(shares, 'head', axis=1, tiled=True)]
    psum x2 -> x0, blocking collectives: 83.6 us -> none  [the longest x1 43.2 us: body(): lax.psum((out_bias_part, gain_part, shift_part), ('dp', 'head'))]
  transfers between devices with their start and end apart: 21 -> 132, of which waited for: 15 -> 68; matrix products, arithmetic and copies ran while one was open for 31% -> 15% of each run, Pallas kernels for 0% -> 41%
where the time goes in v1:
time: 681 us; the launch traced here: 672 us
  Pallas kernels  278 us (41%)
  starting transfers between devices  147 us (22%)
  waiting for transfers between devices  128 us (19%)
  other arithmetic  55.8 us (8%)
  matrix products  34.2 us (5%)
  local copies, waits for them, and re-layouts  25 us (4%)
    pallas_call x5, Pallas kernels, call_rows(): pl.pallas_call(kernel, grid_spec=pltpu.PrefetchScalarGridSpec(num_scalar_...  278 us
    ppermute x104, starting transfers between devices, dp_permute(): return lax.ppermute(values, 'dp', [(i, place(i)) for i in range(dp_size)])  137 us
    ppermute x104, waiting for transfers between devices, dp_permute(): return lax.ppermute(values, 'dp', [(i, place(i)) for i in range(dp_size)])  126 us
    dot_general x10, matrix products, token_grad(): lax.dot_general(left, right, (((0, 1), (0, 1)), ((), ())), preferred_elem...  34.2 us
  transfers between devices with their start and end apart: 132, of which 68 were waited for; matrix products, arithmetic and copies ran while one was open for 15% of the time, Pallas kernels for 41%

profile of v1, /device:TPU:0, one launch (start us, length us, event | category | flops | bytes accessed | tf_op | source)
XLA Modules:
  0.0 672.1 jit_solution(1209895505412982497)
XLA Ops:
  2.9 2.6 broadcast_select_fusion
  13.1 2.3 constant_dynamic-slice_fusion.73
  38.2 2.7 pad_maximum_fusion.1
  40.9 62.5 %attention.1 = (bf16[4,512,512]{2,1,0:T(8,128)(2,1)}, bf16[4,512,512]{2,1,0:T(8,128)(2,1)}, bf16[4,512,512]{2,1,0:T(8,128)(2,1)}, bf16[4,512,512]{2,1,0:T(8,128)...) custom-call(s32[32]{0:T(128)} %pad_add_fusion.starts_ref, ...), custom_call_target="tpu_custom_call" | custom-call | flops 12884901888 | bytes 37447680 | tf_op jit(solution)/shard_map/attention/pallas_call | solution.py:730
  103.4 50.9 %feed.1 = (bf16[4,512,512]{2,1,0:T(8,128)(2,1)}, bf16[4,512,512]{2,1,0:T(8,128)(2,1)}, bf16[4,512,2048]{2,1,0:T(8,128)(2,1)}, bf16[4,512,512]{2,1,0:T(8,128)(2,1...) custom-call(f32[4,512,512]{2,1,0:T(8,128)} %get-tuple-element.52.r2_, ...), custom_call_target="tpu_custom_call" | custom-call | flops 17179869184 | bytes 40200192 | tf_op jit(solution)/shard_map/feed/pallas_call | solution.py:730
  154.3 42.7 %cross_back.1 = (bf16[4,512,512]{2,1,0:T(8,128)(2,1)}, bf16[4,512,512]{2,1,0:T(8,128)(2,1)}, bf16[4,512,512]{2,1,0:T(8,128)(2,1)}, bf16[4,512,512]{2,1,0:T(8,128...) custom-call(s32[32]{0:T(128)} %pad_add_fusion.starts_ref, ...), custom_call_target="tpu_custom_call" | custom-call | flops 9663676416 | bytes 37296128 | tf_op jit(solution)/shard_map/cross_back/pallas_call | solution.py:730
  197.9 4.4 fusion.7
  202.3 36.5 %self_back.1 = (bf16[4,512,512]{2,1,0:T(8,128)(2,1)}, bf16[4,512,512]{2,1,0:T(8,128)(2,1)}, bf16[4,512,512]{2,1,0:T(8,128)(2,1)}, bf16[4,512,512]{2,1,0:T(8,128)(2,1)}, f32[4,8,512]{2,1,0:T(8,128)}) custom-call(s32[32]{0:T(128)} %pad_add_fusion.starts_ref, f32[4,512,512]{2,1,0:T(8,128)} %get-tuple-element.61.dr1_ref, ...), custom_call_target="tpu_custom_call" | custom-call | flops 9663676416 | bytes 26804224 | tf_op jit(solution)/shard_map/self_back/pallas_call | solution.py:730
  241.2 2.9 collective-permute-start.127
  244.1 8.5 %bitcast_convert_fusion = bf16[2048,512]{1,0:T(8,128)(2,1)S(1)} fusion(bf16[4,512,2048]{2,1,0:T(8,128)(2,1)} %get-tuple-element.82, bf16[4,512,512]{2,1,0:T(8,128)(2,1)} %get-tuple-element.83), kind=kOutput, calls=%fused_computation | convolution fusion | flops 4296015872 | bytes 12582912 | tf_op jit(solution)/shard_map/dot_general | solution.py:857
  255.5 8.3 %bitcast_convert_fusion.1 = bf16[512,2048]{1,0:T(8,128)(2,1)S(1)} fusion(bf16[4,512,512]{2,1,0:T(8,128)(2,1)S(1)} %copy-done.59, bf16[4,512,2048]{2,1,0:T(8,128)(2,1)} %get-tuple-element.81), kind=kOutput, calls=%fused_computation.1 | convolution fusion | flops 4296015872 | bytes 12582912 | tf_op jit(solution)/shard_map/dot_general | solution.py:857
  271.4 2.1 fusion
  273.4 2.1 fusion.1
  277.5 2.1 fusion.2
  287.8 85.3 %first_pass.1 = bf16[4,512,512]{2,1,0:T(8,128)(2,1)} custom-call(s32[32]{0:T(128)} %pad_add_fusion.starts_ref, bf16[4,512,512]{2,1,0:T(8,128)(2,1)} %pad_maximum_fusion.x_ref, bf16[4,512,512]{2,1,0:T(8,128)(2,1)} %get-tuple-element.56.k2_ref, bf16[4,512,512]{2,1,0:T(8,128)(2,1)} %get-tuple-element.57.v2_ref, ...), custom_call_target="tpu_custom_call" | custom-call | flops 19327352832 | bytes 17401856 | tf_op jit(solution)/shard_map/first_pass/pallas_call | solution.py:730
  375.0 2.9 fusion.4
  378.8 4.0 collective-permute-done.128
  384.0 2.9 collective-permute-done.129
  386.9 4.2 collective-permute-start.130
  391.2 2.0 collective-permute-done.130
  401.4 2.1 collective-permute-start.73
  404.1 3.2 collective-permute-done.73
  409.0 3.2 collective-permute-done.62
  414.5 2.8 collective-permute-done.51
  437.6 3.1 collective-permute-start.76
  442.6 2.8 collective-permute-start.87
  448.2 2.7 collective-permute-start.65
  453.7 2.8 collective-permute-start.98
  459.2 2.9 collective-permute-start.54
  464.8 2.9 collective-permute-start.21
  470.4 2.8 collective-permute-start.32
  475.9 2.8 collective-permute-start.43
  482.6 2.9 collective-permute-done.44
  485.5 2.1 collective-permute-start.102
  487.6 2.5 collective-permute-done.101
  496.8 2.6 collective-permute-done.80
  499.6 2.0 collective-permute-start.91
  501.6 2.4 collective-permute-done.90
  510.7 2.6 collective-permute-done.69
  515.6 2.4 collective-permute-done.57
  524.7 2.5 collective-permute-done.25
  529.7 2.2 collective-permute-done.35
  543.0 2.7 collective-permute-done.81
  547.0 3.0 collective-permute-done.92
  550.0 2.6 collective-permute-start.26
  552.7 2.9 collective-permute-done.26
  556.6 3.9 collective-permute-done.37
  562.0 2.8 collective-permute-done.48
  571.8 3.8 collective-permute-done.82
  576.2 4.3 collective-permute-done.93
  582.2 3.3 collective-permute-done.71
  591.1 4.3 collective-permute-done.38
  596.5 3.8 collective-permute-done.49
  616.6 2.5 collective-permute-done.117
  623.6 3.5 collective-permute-done.118
  627.2 2.1 collective-permute-start.120
  629.4 2.2 collective-permute-start.121
  631.8 2.1 collective-permute-start.109
  633.9 2.2 collective-permute-start.110
  638.6 2.1 collective-permute-start.124
  641.7 2.7 collective-permute-start.111
  648.2 3.2 collective-permute-done.112
  655.0 5.8 collective-permute-done.114
  664.0 3.9 collective-permute-done.126
  (604 shorter events, 208.5 us)
Async XLA Ops:
  5.6 28.6 %collective-permute-start.1 = (bf16[4,256,512]{2,1,0:T(8,128)(2,1)S(1)}, bf16[4,256,512]{2,1,0:T(8,128)(2,1)}, u32[]{:S(2)}, u32[]{:S(2)}) collective-permute-start(bf16[4,256,512]{2,1,0:T(8,128)(2,1)S(1)} %constant_dynamic-slice_fusion.75), channel_id=1, source_target_pairs={{0,1},{1,0},{2,3},{3,2},{4,5},{5,4},{6,7},{7,6},{8,9},{9,8},{10,11... | collective-permute-start | bytes 3145736 | tf_op jit(solution)/shard_map/ppermute | solution.py:749
  7.2 29.3 %collective-permute-start.2 = (bf16[4,256,512]{2,1,0:T(8,128)(2,1)}, bf16[4,256,512]{2,1,0:T(8,128)(2,1)}, u32[]{:S(2)}, u32[]{:S(2)}) collective-permute-start(bf16[4,256,512]{2,1,0:T(8,128)(2,1)} %constant_dynamic-slice_fusion.74), channel_id=1, source_target_pairs={{0,1},{1,0},{2,3},{3,2},{4,5},{5,4},{6,7},{7,6},{8,9},{9,8},{10,11... | collective-permute-start | bytes 3145736 | tf_op jit(solution)/shard_map/ppermute | solution.py:749
  7.6 13.2 %collective-permute-start.4 = (bf16[256,512]{1,0:T(8,128)(2,1)}, bf16[256,512]{1,0:T(8,128)(2,1)}, u32[]{:S(2)}, u32[]{:S(2)}) collective-permute-start(bf16[256,512]{1,0:T(8,128)(2,1)} %param.33), channel_id=1, source_target_pairs={{0,1},{1,0},{2,3},{3,2},{4,5},{5,4},{6,7},{7,6},{8,9},{9,8},{10,11... | collective-permute-start | bytes 786440 | tf_op jit(solution)/shard_map/ppermute | solution.py:749
  7.7 13.2 %collective-permute-start.7 = (bf16[256,512]{1,0:T(8,128)(2,1)S(1)}, bf16[256,512]{1,0:T(8,128)(2,1)}, u32[]{:S(2)}, u32[]{:S(2)}) collective-permute-start(bf16[256,512]{1,0:T(8,128)(2,1)S(1)} %copy-done.44), channel_id=1, source_target_pairs={{0,1},{1,0},{2,3},{3,2},{4,5},{5,4},{6,7},{7,6},{8,9},{9,8},{10,11... | collective-permute-start | bytes 786440 | tf_op jit(solution)/shard_map/ppermute | solution.py:749
  8.1 9.7 %collective-permute-start.8 = (bf16[4,256]{1,0:T(4,128)(2,1)S(1)}, bf16[4,256]{1,0:T(4,128)(2,1)S(1)}, u32[]{:S(2)}, u32[]{:S(2)}) collective-permute-start(bf16[4,256]{1,0:T(4,128)(2,1)S(1)} %copy-done.52), channel_id=1, source_target_pairs={{0,1},{1,0},{2,3},{3,2},{4,5},{5,4},{6,7},{7,6},{8,9},{9,8},{10,11... | collective-permute-start | bytes 6152 | tf_op jit(solution)/shard_map/ppermute | solution.py:749
  19.1 7.7 %collective-permute-start.3 = (bf16[3,512,256]{2,1,0:T(8,128)(2,1)}, bf16[3,512,256]{2,1,0:T(8,128)(2,1)S(1)}, u32[]{:S(2)}, u32[]{:S(2)}) collective-permute-start(bf16[3,512,256]{2,1,0:T(8,128)(2,1)} %param.32), channel_id=1, source_target_pairs={{0,1},{1,0},{2,3},{3,2},{4,5},{5,4},{6,7},{7,6},{8,9},{9,8},{10,11... | collective-permute-start | bytes 2359304 | tf_op jit(solution)/shard_map/ppermute | solution.py:749
  22.5 5.9 collective-permute-start.9
  26.8 5.7 collective-permute-start.11
  28.4 252.6 %collective-permute-start = (bf16[4,256,512]{2,1,0:T(8,128)(2,1)}, bf16[4,256,512]{2,1,0:T(8,128)(2,1)}, u32[]{:S(2)}, u32[]{:S(2)}) collective-permute-start(bf16[4,256,512]{2,1,0:T(8,128)(2,1)} %constant_dynamic-slice_fusion.78), channel_id=1, source_target_pairs={{0,1},{1,0},{2,3},{3,2},{4,5},{5,4},{6,7},{7,6},{8,9},{9,8},{10,11... | collective-permute-start | bytes 3145736 | tf_op jit(solution)/shard_map/ppermute | solution.py:749
  241.2 136.8 %collective-permute-start.127 = (f32[17,512]{1,0:T(8,128)S(1)}, f32[17,512]{1,0:T(8,128)S(1)}, u32[]{:S(2)}, u32[]{:S(2)}) collective-permute-start(f32[17,512]{1,0:T(8,128)S(1)} %concatenate.83), channel_id=1, source_target_pairs={{0,2},{2,0},{4,6},{6,4},{8,10},{10,8},{12,14},{14,12},{16,18},{18,... | collective-permute-start | bytes 104456 | tf_op jit(solution)/shard_map/ppermute | solution.py:810
  253.8 348.9 %collective-permute-start.116 = (bf16[1024,512]{1,0:T(8,128)(2,1)}, bf16[1024,512]{1,0:T(8,128)(2,1)}, u32[]{:S(2)}, u32[]{:S(2)}) collective-permute-start(bf16[1024,512]{1,0:T(8,128)(2,1)} %constant_dynamic-slice_fusion.6), channel_id=1, source_target_pairs={{0,1},{1,0},{2,3},{3,2},{4,5},{5,4},{6,7},{7,6},{8,9},{9,8},{10,11... | collective-permute-start | bytes 3145736 | tf_op jit(solution)/shard_map/ppermute | solution.py:749
  264.9 340.1 %collective-permute-start.105 = (bf16[512,1024]{1,0:T(8,128)(2,1)}, bf16[512,1024]{1,0:T(8,128)(2,1)}, u32[]{:S(2)}, u32[]{:S(2)}) collective-permute-start(bf16[512,1024]{1,0:T(8,128)(2,1)} %constant_dynamic-slice_fusion.12), channel_id=1, source_target_pairs={{0,1},{1,0},{2,3},{3,2},{4,5},{5,4},{6,7},{7,6},{8,9},{9,8},{10,11... | collective-permute-start | bytes 3145736 | tf_op jit(solution)/shard_map/ppermute | solution.py:749
  267.2 129.3 %collective-permute-start.94 = (bf16[256,512]{1,0:T(8,128)(2,1)}, bf16[256,512]{1,0:T(8,128)(2,1)}, u32[]{:S(2)}, u32[]{:S(2)}) collective-permute-start(bf16[256,512]{1,0:T(8,128)(2,1)} %constant_dynamic-slice_fusion.19), channel_id=1, source_target_pairs={{0,1},{1,0},{2,3},{3,2},{4,5},{5,4},{6,7},{7,6},{8,9},{9,8},{10,11... | collective-permute-start | bytes 786440 | tf_op jit(solution)/shard_map/ppermute | solution.py:749
  281.0 116.9 %collective-permute-start.72 = (bf16[512,256]{1,0:T(8,128)(2,1)}, bf16[512,256]{1,0:T(8,128)(2,1)}, u32[]{:S(2)}, u32[]{:S(2)}) collective-permute-start(bf16[512,256]{1,0:T(8,128)(2,1)} %constant_dynamic-slice_fusion.33), channel_id=1, source_target_pairs={{0,1},{1,0},{2,3},{3,2},{4,5},{5,4},{6,7},{7,6},{8,9},{9,8},{10,11... | collective-permute-start | bytes 786440 | tf_op jit(solution)/shard_map/ppermute | solution.py:749
  386.9 6.3 collective-permute-start.130
  400.7 12.7 %collective-permute-start.95 = (bf16[128,512]{1,0:T(8,128)(2,1)S(1)}, bf16[128,512]{1,0:T(8,128)(2,1)S(1)}, u32[]{:S(2)}, u32[]{:S(2)}) collective-permute-start(bf16[128,512]{1,0:T(8,128)(2,1)S(1)} %constant_dynamic-slice_fusion.18), channel_id=1, source_target_pairs={{0,4},{2,6},{4,0},{6,2},{8,12},{10,14},{12,8},{14,10},{16,20},{18,... | collective-permute-start | bytes 393224 | tf_op jit(solution)/shard_map/ppermute | solution.py:810
  401.4 5.9 collective-permute-start.73
  403.6 16.6 %collective-permute-start.84 = (bf16[256,256]{1,0:T(8,128)(2,1)S(1)}, bf16[256,256]{1,0:T(8,128)(2,1)S(1)}, u32[]{:S(2)}, u32[]{:S(2)}) collective-permute-start(bf16[256,256]{1,0:T(8,128)(2,1)S(1)} %constant_dynamic-slice_fusion.25), channel_id=1, source_target_pairs={{0,4},{2,6},{4,0},{6,2},{8,12},{10,14},{12,8},{14,10},{16,20},{18,... | collective-permute-start | bytes 393224 | tf_op jit(solution)/shard_map/ppermute | solution.py:810
  413.5 5.8 collective-permute-start.18
  417.3 5.7 collective-permute-start.29
  420.2 13.0 %collective-permute-start.96 = (bf16[64,512]{1,0:T(8,128)(2,1)S(1)}, bf16[64,512]{1,0:T(8,128)(2,1)S(1)}, u32[]{:S(2)}, u32[]{:S(2)}) collective-permute-start(bf16[64,512]{1,0:T(8,128)(2,1)S(1)} %constant_dynamic-slice_fusion.17), channel_id=1, source_target_pairs={{0,2},{2,0},{4,6},{6,4},{8,10},{10,8},{12,14},{14,12},{16,18},{18,... | collective-permute-start | bytes 196616 | tf_op jit(solution)/shard_map/ppermute | solution.py:810
  434.0 6.8 %collective-permute-start.41 = (bf16[128,256]{1,0:T(8,128)(2,1)S(1)}, bf16[128,256]{1,0:T(8,128)(2,1)S(1)}, u32[]{:S(2)}, u32[]{:S(2)}) collective-permute-start(bf16[128,256]{1,0:T(8,128)(2,1)S(1)} %constant_dynamic-slice_fusion.52), channel_id=1, source_target_pairs={{0,4},{2,6},{4,0},{6,2},{8,12},{10,14},{12,8},{14,10},{16,20},{18,... | collective-permute-start | bytes 196616 | tf_op jit(solution)/shard_map/ppermute | solution.py:810
  436.0 6.3 collective-permute-start.75
  440.8 5.6 collective-permute-start.77
  442.4 5.7 collective-permute-start.86
  442.6 5.6 collective-permute-start.87
  446.4 5.6 collective-permute-start.88
  452.0 5.6 collective-permute-start.66
  464.7 5.6 collective-permute-start.20
  464.8 5.6 collective-permute-start.21
  468.7 5.6 collective-permute-start.22
  479.8 5.7 collective-permute-start.44
  481.4 126.1 %collective-permute-start.16 = (bf16[4,256,512]{2,1,0:T(8,128)(2,1)S(1)}, bf16[4,256,512]{2,1,0:T(8,128)(2,1)S(1)}, u32[]{:S(2)}, u32[]{:S(2)}) collective-permute-start(bf16[4,256,512]{2,1,0:T(8,128)(2,1)S(1)} %copy-done.31), channel_id=1, source_target_pairs={{0,1},{1,0},{2,3},{3,2},{4,5},{5,4},{6,7},{7,6},{8,9},{9,8},{10,11... | collective-permute-start | bytes 3145736 | tf_op jit(solution)/shard_map/ppermute | solution.py:749
  485.5 5.6 collective-permute-start.102
  493.9 5.5 collective-permute-start.80
  499.6 5.6 collective-permute-start.91
  513.6 5.7 collective-permute-start.58
  538.1 28.1 %collective-permute-start.103 = (bf16[64,512]{1,0:T(8,128)(2,1)S(1)}, bf16[64,512]{1,0:T(8,128)(2,1)S(1)}, u32[]{:S(2)}, u32[]{:S(2)}) collective-permute-start(bf16[64,512]{1,0:T(8,128)(2,1)S(1)} %constant_dynamic-update-slice_fusion.20), channel_id=1, source_target_pairs={{0,2},{2,0},{4,6},{6,4},{8,10},{10,8},{12,14},{14,12},{16,18},{18,... | collective-permute-start | bytes 196616 | tf_op jit(solution)/shard_map/ppermute | solution.py:810
  550.0 5.6 collective-permute-start.26
  569.0 12.6 %collective-permute-start.104 = (bf16[128,512]{1,0:T(8,128)(2,1)S(1)}, bf16[128,512]{1,0:T(8,128)(2,1)S(1)}, u32[]{:S(2)}, u32[]{:S(2)}) collective-permute-start(bf16[128,512]{1,0:T(8,128)(2,1)S(1)} %constant_dynamic-update-slice_fusion.18), channel_id=1, source_target_pairs={{0,4},{2,6},{4,0},{6,2},{8,12},{10,14},{12,8},{14,10},{16,20},{18,... | collective-permute-start | bytes 393224 | tf_op jit(solution)/shard_map/ppermute | solution.py:810
  581.6 6.6 collective-permute-start.60
  588.3 22.2 %collective-permute-start.15 = (bf16[4,256,512]{2,1,0:T(8,128)(2,1)S(1)}, bf16[4,256,512]{2,1,0:T(8,128)(2,1)S(1)}, u32[]{:S(2)}, u32[]{:S(2)}) collective-permute-start(bf16[4,256,512]{2,1,0:T(8,128)(2,1)S(1)} %copy-done.33), channel_id=1, source_target_pairs={{0,1},{1,0},{2,3},{3,2},{4,5},{5,4},{6,7},{7,6},{8,9},{9,8},{10,11... | collective-permute-start | bytes 3145736 | tf_op jit(solution)/shard_map/ppermute | solution.py:749
  600.4 11.4 %collective-permute-start.14 = (bf16[4,256,512]{2,1,0:T(8,128)(2,1)S(1)}, bf16[4,256,512]{2,1,0:T(8,128)(2,1)S(1)}, u32[]{:S(2)}, u32[]{:S(2)}) collective-permute-start(bf16[4,256,512]{2,1,0:T(8,128)(2,1)S(1)} %copy-done.32), channel_id=1, source_target_pairs={{0,1},{1,0},{2,3},{3,2},{4,5},{5,4},{6,7},{7,6},{8,9},{9,8},{10,11... | collective-permute-start | bytes 3145736 | tf_op jit(solution)/shard_map/ppermute | solution.py:749
  602.7 11.1 %collective-permute-start.13 = (bf16[4,256,512]{2,1,0:T(8,128)(2,1)S(1)}, bf16[4,256,512]{2,1,0:T(8,128)(2,1)S(1)}, u32[]{:S(2)}, u32[]{:S(2)}) collective-permute-start(bf16[4,256,512]{2,1,0:T(8,128)(2,1)S(1)} %constant_dynamic-slice_fusion.72), channel_id=1, source_target_pairs={{0,1},{1,0},{2,3},{3,2},{4,5},{5,4},{6,7},{7,6},{8,9},{9,8},{10,11... | collective-permute-start | bytes 3145736 | tf_op jit(solution)/shard_map/ppermute | solution.py:749
  605.1 14.1 %collective-permute-start.117 = (bf16[512,512]{1,0:T(8,128)(2,1)S(1)}, bf16[512,512]{1,0:T(8,128)(2,1)S(1)}, u32[]{:S(2)}, u32[]{:S(2)}) collective-permute-start(bf16[512,512]{1,0:T(8,128)(2,1)S(1)} %constant_dynamic-slice_fusion.5), channel_id=1, source_target_pairs={{0,4},{2,6},{4,0},{6,2},{8,12},{10,14},{12,8},{14,10},{16,20},{18,... | collective-permute-start | bytes 1572872 | tf_op jit(solution)/shard_map/ppermute | solution.py:810
  607.4 14.0 %collective-permute-start.106 = (bf16[256,1024]{1,0:T(8,128)(2,1)S(1)}, bf16[256,1024]{1,0:T(8,128)(2,1)S(1)}, u32[]{:S(2)}, u32[]{:S(2)}) collective-permute-start(bf16[256,1024]{1,0:T(8,128)(2,1)S(1)} %constant_dynamic-slice_fusion.11), channel_id=1, source_target_pairs={{0,2},{2,0},{4,6},{6,4},{8,10},{10,8},{12,14},{14,12},{16,18},{18,... | collective-permute-start | bytes 1572872 | tf_op jit(solution)/shard_map/ppermute | solution.py:810
  619.3 7.7 %collective-permute-start.118 = (bf16[256,512]{1,0:T(8,128)(2,1)S(1)}, bf16[256,512]{1,0:T(8,128)(2,1)S(1)}, u32[]{:S(2)}, u32[]{:S(2)}) collective-permute-start(bf16[256,512]{1,0:T(8,128)(2,1)S(1)} %constant_dynamic-slice_fusion.4), channel_id=1, source_target_pairs={{0,2},{2,0},{4,6},{6,4},{8,10},{10,8},{12,14},{14,12},{16,18},{18,... | collective-permute-start | bytes 786440 | tf_op jit(solution)/shard_map/ppermute | solution.py:810
  621.7 9.9 %collective-permute-start.107 = (bf16[128,1024]{1,0:T(8,128)(2,1)S(1)}, bf16[128,1024]{1,0:T(8,128)(2,1)S(1)}, u32[]{:S(2)}, u32[]{:S(2)}) collective-permute-start(bf16[128,1024]{1,0:T(8,128)(2,1)S(1)} %constant_dynamic-slice_fusion.10), channel_id=1, source_target_pairs={{0,4},{2,6},{4,0},{6,2},{8,12},{10,14},{12,8},{14,10},{16,20},{18,... | collective-permute-start | bytes 786440 | tf_op jit(solution)/shard_map/ppermute | solution.py:810
  627.1 6.8 %collective-permute-start.119 = (bf16[64,512]{1,0:T(8,128)(2,1)S(1)}, bf16[64,512]{1,0:T(8,128)(2,1)S(1)}, u32[]{:S(2)}, u32[]{:S(2)}) collective-permute-start(bf16[64,512]{1,0:T(8,128)(2,1)S(1)} %get-tuple-element.146), channel_id=1, source_target_pairs={{0,8},{2,10},{4,12},{6,14},{8,0},{10,2},{12,4},{14,6},{16,24},{18,... | collective-permute-start | bytes 196616 | tf_op jit(solution)/shard_map/ppermute | solution.py:810
  627.2 8.9 %collective-permute-start.120 = (bf16[64,512]{1,0:T(8,128)(2,1)S(1)}, bf16[64,512]{1,0:T(8,128)(2,1)S(1)}, u32[]{:S(2)}, u32[]{:S(2)}) collective-permute-start(bf16[64,512]{1,0:T(8,128)(2,1)S(1)} %get-tuple-element.148), channel_id=1, source_target_pairs={{0,16},{2,18},{4,20},{6,22},{8,24},{10,26},{12,28},{14,30},{16,0},... | collective-permute-start | bytes 196616 | tf_op jit(solution)/shard_map/ppermute | solution.py:810
  629.4 6.8 %collective-permute-start.121 = (bf16[64,512]{1,0:T(8,128)(2,1)S(1)}, bf16[64,512]{1,0:T(8,128)(2,1)S(1)}, u32[]{:S(2)}, u32[]{:S(2)}) collective-permute-start(bf16[64,512]{1,0:T(8,128)(2,1)S(1)} %get-tuple-element.147), channel_id=1, source_target_pairs={{0,24},{2,26},{4,28},{6,30},{8,16},{10,18},{12,20},{14,22},{16,8},... | collective-permute-start | bytes 196616 | tf_op jit(solution)/shard_map/ppermute | solution.py:810
  631.7 6.9 %collective-permute-start.108 = (bf16[32,1024]{1,0:T(8,128)(2,1)S(1)}, bf16[32,1024]{1,0:T(8,128)(2,1)S(1)}, u32[]{:S(2)}, u32[]{:S(2)}) collective-permute-start(bf16[32,1024]{1,0:T(8,128)(2,1)S(1)} %get-tuple-element.149), channel_id=1, source_target_pairs={{0,8},{2,10},{4,12},{6,14},{8,0},{10,2},{12,4},{14,6},{16,24},{18,... | collective-permute-start | bytes 196616 | tf_op jit(solution)/shard_map/ppermute | solution.py:810
  631.8 9.8 %collective-permute-start.109 = (bf16[32,1024]{1,0:T(8,128)(2,1)S(1)}, bf16[32,1024]{1,0:T(8,128)(2,1)S(1)}, u32[]{:S(2)}, u32[]{:S(2)}) collective-permute-start(bf16[32,1024]{1,0:T(8,128)(2,1)S(1)} %get-tuple-element.151), channel_id=1, source_target_pairs={{0,16},{2,18},{4,20},{6,22},{8,24},{10,26},{12,28},{14,30},{16,0},... | collective-permute-start | bytes 196616 | tf_op jit(solution)/shard_map/ppermute | solution.py:810
  633.9 7.7 %collective-permute-start.110 = (bf16[32,1024]{1,0:T(8,128)(2,1)S(1)}, bf16[32,1024]{1,0:T(8,128)(2,1)S(1)}, u32[]{:S(2)}, u32[]{:S(2)}) collective-permute-start(bf16[32,1024]{1,0:T(8,128)(2,1)S(1)} %get-tuple-element.150), channel_id=1, source_target_pairs={{0,24},{2,26},{4,28},{6,30},{8,16},{10,18},{12,20},{14,22},{16,8},... | collective-permute-start | bytes 196616 | tf_op jit(solution)/shard_map/ppermute | solution.py:810
  636.2 8.7 %collective-permute-start.122 = (bf16[64,512]{1,0:T(8,128)(2,1)S(1)}, bf16[64,512]{1,0:T(8,128)(2,1)S(1)}, u32[]{:S(2)}, u32[]{:S(2)}) collective-permute-start(bf16[64,512]{1,0:T(8,128)(2,1)S(1)} %get-tuple-element.97), channel_id=1, source_target_pairs={{0,8},{2,10},{4,12},{6,14},{8,0},{10,2},{12,4},{14,6},{16,24},{18,... | collective-permute-start | bytes 196616 | tf_op jit(solution)/shard_map/ppermute | solution.py:810
  638.1 8.8 %collective-permute-start.123 = (bf16[64,512]{1,0:T(8,128)(2,1)S(1)}, bf16[64,512]{1,0:T(8,128)(2,1)S(1)}, u32[]{:S(2)}, u32[]{:S(2)}) collective-permute-start(bf16[64,512]{1,0:T(8,128)(2,1)S(1)} %get-tuple-element.97), channel_id=1, source_target_pairs={{0,16},{2,18},{4,20},{6,22},{8,24},{10,26},{12,28},{14,30},{16,0},... | collective-permute-start | bytes 196616 | tf_op jit(solution)/shard_map/ppermute | solution.py:810
  638.6 8.3 %collective-permute-start.124 = (bf16[64,512]{1,0:T(8,128)(2,1)S(1)}, bf16[64,512]{1,0:T(8,128)(2,1)S(1)}, u32[]{:S(2)}, u32[]{:S(2)}) collective-permute-start(bf16[64,512]{1,0:T(8,128)(2,1)S(1)} %get-tuple-element.97), channel_id=1, source_target_pairs={{0,24},{2,26},{4,28},{6,30},{8,16},{10,18},{12,20},{14,22},{16,8},... | collective-permute-start | bytes 196616 | tf_op jit(solution)/shard_map/ppermute | solution.py:810
  641.7 6.5 collective-permute-start.111
  644.4 7.0 %collective-permute-start.112 = (bf16[32,1024]{1,0:T(8,128)(2,1)S(1)}, bf16[32,1024]{1,0:T(8,128)(2,1)S(1)}, u32[]{:S(2)}, u32[]{:S(2)}) collective-permute-start(bf16[32,1024]{1,0:T(8,128)(2,1)S(1)} %get-tuple-element.99), channel_id=1, source_target_pairs={{0,16},{2,18},{4,20},{6,22},{8,24},{10,26},{12,28},{14,30},{16,0},... | collective-permute-start | bytes 196616 | tf_op jit(solution)/shard_map/ppermute | solution.py:810
  644.9 6.5 collective-permute-start.113
  646.9 6.4 collective-permute-start.125
  651.5 9.3 %collective-permute-start.114 = (bf16[128,1024]{1,0:T(8,128)(2,1)S(1)}, bf16[128,1024]{1,0:T(8,128)(2,1)S(1)}, u32[]{:S(2)}, u32[]{:S(2)}) collective-permute-start(bf16[128,1024]{1,0:T(8,128)(2,1)S(1)} %constant_dynamic-update-slice_fusion.12), channel_id=1, source_target_pairs={{0,4},{2,6},{4,0},{6,2},{8,12},{10,14},{12,8},{14,10},{16,20},{18,... | collective-permute-start | bytes 786440 | tf_op jit(solution)/shard_map/ppermute | solution.py:810
  653.4 14.6 %collective-permute-start.126 = (bf16[512,512]{1,0:T(8,128)(2,1)S(1)}, bf16[512,512]{1,0:T(8,128)(2,1)S(1)}, u32[]{:S(2)}, u32[]{:S(2)}) collective-permute-start(bf16[512,512]{1,0:T(8,128)(2,1)S(1)} %constant_dynamic-update-slice_fusion.2), channel_id=1, source_target_pairs={{0,4},{2,6},{4,0},{6,2},{8,12},{10,14},{12,8},{14,10},{16,20},{18,... | collective-permute-start | bytes 1572872 | tf_op jit(solution)/shard_map/ppermute | solution.py:810
  660.8 9.2 %collective-permute-start.115 = (bf16[256,1024]{1,0:T(8,128)(2,1)S(1)}, bf16[256,1024]{1,0:T(8,128)(2,1)S(1)}, u32[]{:S(2)}, u32[]{:S(2)}) collective-permute-start(bf16[256,1024]{1,0:T(8,128)(2,1)S(1)} %constant_dynamic-update-slice_fusion.10), channel_id=1, source_target_pairs={{0,2},{2,0},{4,6},{6,4},{8,10},{10,8},{12,14},{14,12},{16,18},{18,... | collective-permute-start | bytes 1572872 | tf_op jit(solution)/shard_map/ppermute | solution.py:810
  (128 other events, 720.2 us)

commit v2 on v0

v2 whole, which is shorter than its diff:
```python
import functools

import jax
import jax.numpy as jnp
import numpy as np
from jax import lax
from jax.experimental import pallas as pl
from jax.experimental.pallas import tpu as pltpu
from jax.sharding import PartitionSpec as P

HEAD_DIM = 64
PAIR = 2 * HEAD_DIM
TILE = 128
WINDOW = 256
FAR = -1e30
F32 = jnp.float32
BF16 = jnp.bfloat16
VMEM_BYTES = 60 * 1024 * 1024


def dot_nn(left, right):
    return lax.dot_general(left, right, (((1,), (0,)), ((), ())), preferred_element_type=F32)


def dot_nt(left, right):
    return lax.dot_general(left, right, (((1,), (1,)), ((), ())), preferred_element_type=F32)


def norm_stats(sums):
    row_mean = jnp.mean(sums, axis=-1, keepdims=True)
    centred = sums - row_mean
    spread = jnp.mean(centred * centred, axis=-1, keepdims=True)
    inverse = lax.rsqrt(spread + 1e-05)
    return centred * inverse, inverse


def norm_back(normed, inverse, gain_row, incoming):
    scaled = incoming * gain_row
    mean_one = jnp.mean(scaled, axis=-1, keepdims=True)
    mean_two = jnp.mean(scaled * normed, axis=-1, keepdims=True)
    grad = (scaled - mean_one - normed * mean_two) * inverse
    gain_part = jnp.sum(incoming * normed, axis=0, keepdims=True)
    shift_part = jnp.sum(incoming, axis=0, keepdims=True)
    return grad, gain_part, shift_part


def gelu_parts(pre):
    ratio = pltpu.reciprocal(1.0 + 0.23164189015488 * jnp.abs(pre), approx=True)
    series = ratio * (
        0.127414796
        + ratio
        * (-0.142248368 + ratio * (0.7107068705 + ratio * (-0.7265760135 + ratio * 0.5307027145)))
    )
    bell = jnp.exp(-0.5 * (pre * pre))
    tail = series * bell
    return jnp.where(pre >= 0, 1.0 - tail, tail), bell


def each_tile(count, step):
    def one(index, carry):
        step(index)
        return carry

    lax.fori_loop(0, count, one, 0)


def tile_rows(tile):
    start = tile * TILE
    return pl.ds(start if isinstance(start, int) else pl.multiple_of(start, TILE), TILE)


def window_loop(starts_ref, base, tiles, length, step):
    starts = [starts_ref[base + tile] for tile in range(tiles)]
    least = functools.reduce(jnp.minimum, starts)
    window = min(WINDOW, length)

    @pl.when(least >= 0)
    def straight():
        for tile in range(tiles):
            step(tile, pl.multiple_of(starts[tile], 16), window)

    if length > WINDOW:

        @pl.when(least < 0)
        def mixed():
            def one(tile):
                start = starts_ref[base + tile]

                @pl.when(start >= 0)
                def near():
                    step(tile, pl.multiple_of(start, 16), window)

                @pl.when(start < 0)
                def whole():
                    step(tile, 0, length)

            each_tile(tiles, one)


def make_marks(segment_row, levels, heads):
    shape = (PAIR, segment_row.shape[1])
    level = lax.broadcasted_iota(jnp.int32, shape, 0)
    same = level == segment_row
    near = jnp.where(same | ((level >= 16) & (level < 16 + 3 * heads)), 1.0, 0.0)
    far = jnp.where(same | (level >= levels), 0.0, FAR)
    return far.T.astype(BF16), near.T.astype(BF16)


def attend(q_ref, k_ref, v_ref, far_ref, near_ref, sides_ref, ctx_ref, lse_ref, starts_ref, base):
    length, width = q_ref.shape
    pairs = range(width // PAIR)
    lanes = [slice(p * PAIR, (p + 1) * PAIR) for p in pairs]

    def step(tile, start, window):
        rows = tile_rows(tile)
        keys = pl.ds(start, window)
        left, right = sides_ref[0], sides_ref[1]
        query_marks = far_ref[rows, :]
        key_marks = near_ref[keys, :]
        stacked = []
        for p in pairs:
            queries = q_ref[rows, lanes[p]]
            stacked.append(
                jnp.concatenate(
                    [
                        jnp.concatenate([queries * left, query_marks], axis=1),
                        jnp.concatenate([queries * right, query_marks], axis=1),
                    ],
                    axis=0,
                )
            )
        scores = [
            dot_nt(jnp.concatenate([k_ref[keys, lanes[p]], key_marks], axis=1), stacked[p])
            for p in pairs
        ]
        peaks = [jnp.max(s, axis=0, keepdims=True) for s in scores]
        weights = [jnp.exp(s - m) for s, m in zip(scores, peaks)]
        totals = [jnp.sum(w, axis=0, keepdims=True) for w in weights]
        low = [w.astype(BF16) for w in weights]
        turned = [v_ref[keys, lanes[p]].T for p in pairs]
        mixed = [dot_nn(turned[p], low[p]) for p in pairs]
        shares = [pltpu.reciprocal(t, approx=True) for t in totals]
        context = [
            jnp.concatenate(
                [
                    mixed[p][:HEAD_DIM, :TILE] * shares[p][:, :TILE],
                    mixed[p][HEAD_DIM:, TILE:] * shares[p][:, TILE:],
                ],
                axis=0,
            )
            for p in pairs
        ]
        for p in pairs:
            ctx_ref[rows, lanes[p]] = context[p].T.astype(BF16)
        if lse_ref is not None:
            for p in pairs:
                log_total = peaks[p] + jnp.log(totals[p])
                lse_ref[tile, pl.ds(2 * p, 1), :] = log_total[:, :TILE]
                lse_ref[tile, pl.ds(2 * p + 1, 1), :] = log_total[:, TILE:]

    window_loop(starts_ref, base, length // TILE, length, step)


def three_parts(values):
    high = values.astype(BF16).astype(F32)
    rest = values - high
    middle = rest.astype(BF16).astype(F32)
    return high, middle, rest - middle


def attend_back(
    q_ref,
    k_ref,
    v_ref,
    far_ref,
    near_ref,
    sides_ref,
    own_ref,
    spread_ref,
    lse_ref,
    ctx_ref,
    dctx_ref,
    dq_ref,
    dk_ref,
    dv_ref,
    starts_ref,
    base,
):
    length, width = q_ref.shape
    pairs = range(width // PAIR)
    heads = width // HEAD_DIM
    lanes = [slice(p * PAIR, (p + 1) * PAIR) for p in pairs]
    dk_ref[...] = jnp.zeros_like(dk_ref)
    dv_ref[...] = jnp.zeros_like(dv_ref)

    def step(tile, start, window):
        rows = tile_rows(tile)
        keys = pl.ds(start, window)
        left, right = sides_ref[0], sides_ref[1]
        key_marks = near_ref[keys, :]
        high, middle, rest = three_parts(-lse_ref[tile])
        stats = jnp.concatenate(
            [
                jnp.zeros((16, TILE), F32),
                high,
                middle,
                rest,
                jnp.zeros((TILE - 16 - 3 * heads, TILE), F32),
            ],
            axis=0,
        )
        query_marks = far_ref[rows, :] + stats.T.astype(BF16)
        product = dctx_ref[rows, :].astype(F32) * ctx_ref[rows, :].astype(F32)
        product_high = product.astype(BF16)
        product_rest = (product - product_high.astype(F32)).astype(BF16)
        delta = -(dot_nn(product_high, spread_ref[...]) + dot_nn(product_rest, spread_ref[...]))
        high, middle, rest = three_parts(delta)
        lane = lax.broadcasted_iota(jnp.int32, delta.shape, 1)
        grad_marks = jnp.where(
            lane < 16 + heads, high, jnp.where(lane < 16 + 2 * heads, middle, rest)
        ).astype(BF16)
        query_stack, grad_stack, query_side, grad_side, key_rows = [], [], [], [], []
        for p in pairs:
            queries = q_ref[rows, lanes[p]]
            grads = dctx_ref[rows, lanes[p]]
            key_rows.append(k_ref[keys, lanes[p]])
            query_stack.append(jnp.concatenate([queries * left, queries * right], axis=0))
            grad_stack.append(jnp.concatenate([grads * left, grads * right], axis=0))
            one, two = own_ref[2 * p], own_ref[2 * p + 1]
            marks = jnp.concatenate([query_marks * one, query_marks * two], axis=0)
            query_side.append(jnp.concatenate([query_stack[p], marks], axis=1))
            marks = jnp.concatenate([grad_marks * one, grad_marks * two], axis=0)
            grad_side.append(jnp.concatenate([grad_stack[p], marks], axis=1))
        scores = [
            dot_nt(jnp.concatenate([key_rows[p], key_marks], axis=1), query_side[p]) for p in pairs
        ]
        probs_grad = [
            dot_nt(jnp.concatenate([v_ref[keys, lanes[p]], key_marks], axis=1), grad_side[p])
            for p in pairs
        ]
        probs = [jnp.exp(s) for s in scores]
        probs_low = [w.astype(BF16) for w in probs]
        scores_grad = [(probs[p] * probs_grad[p]).astype(BF16) for p in pairs]
        turned_keys = [key_rows[p].T for p in pairs]
        for p in pairs:
            dv_ref[keys, lanes[p]] += dot_nn(probs_low[p], grad_stack[p])
        for p in pairs:
            dk_ref[keys, lanes[p]] += dot_nn(scores_grad[p], query_stack[p])
        turned = [dot_nn(turned_keys[p], scores_grad[p]) for p in pairs]
        for p in pairs:
            both = jnp.concatenate(
                [turned[p][:HEAD_DIM, :TILE], turned[p][HEAD_DIM:, TILE:]], axis=0
            )
            dq_ref[rows, lanes[p]] = (both.T * (HEAD_DIM**-0.5)).astype(BF16)

    window_loop(starts_ref, base, length // TILE, length, step)


def self_part(
    r, x_ref, seg_ref, near_ref, far_ref, q_ref, k_ref, v_ref, ctx_ref, lse_ref, r1_ref, a1_ref, work_ref, levels
):
    tiles, width = x_ref.shape[0] // TILE, x_ref.shape[1]
    far, near = make_marks(seg_ref[...], levels, width // HEAD_DIM)
    far_ref[...] = far
    near_ref[...] = near
    bias = r.head_bias[...].astype(F32)
    inputs = x_ref[...]
    queries = (dot_nn(inputs, r.self_qkv[0]) + bias[0:1, :]).astype(BF16)
    q_ref[...] = queries * jnp.asarray(HEAD_DIM**-0.5, BF16)
    k_ref[...] = dot_nn(inputs, r.self_qkv[1]).astype(BF16)
    v_ref[...] = (dot_nn(inputs, r.self_qkv[2]) + bias[1:2, :]).astype(BF16)
    base = pl.program_id(0) * tiles
    attend(q_ref, k_ref, v_ref, far_ref, near_ref, r.sides, ctx_ref, lse_ref, r.starts, base)
    work_ref[...] = dot_nn(ctx_ref[...], r.self_out[...])
    out_bias = r.out_bias[0:1, :].astype(F32)
    gain, shift = r.gain[0:1, :].astype(F32), r.shift[0:1, :].astype(F32)

    def step(tile):
        rows = tile_rows(tile)
        sums = x_ref[rows, :].astype(F32) + (work_ref[rows, :] + out_bias)
        if r1_ref is not None:
            r1_ref[rows, :] = sums
        normed = norm_stats(sums)[0] * gain + shift
        work_ref[rows, :] = normed
        a1_ref[rows, :] = normed.astype(BF16)

    each_tile(tiles, step)


def cross_part(
    r, seg_ref, near_ref, far_ref, a1_ref, q2_ref, k2_ref, v2_ref, ctx2_ref, lse2_ref, r2_ref, work_ref, levels
):
    tiles, width = q2_ref.shape[0] // TILE, q2_ref.shape[1]
    near_ref[...] = make_marks(seg_ref[...], levels, width // HEAD_DIM)[1]
    bias = r.head_bias[...].astype(F32)
    queries = (dot_nn(a1_ref[...], r.cross_q[...]) + bias[2:3, :]).astype(BF16)
    q2_ref[...] = queries * jnp.asarray(HEAD_DIM**-0.5, BF16)
    base = (pl.num_programs(0) + pl.program_id(0)) * tiles
    attend(q2_ref, k2_ref, v2_ref, far_ref, near_ref, r.sides, ctx2_ref, lse2_ref, r.starts, base)
    r2_ref[...] = work_ref[...] + (
        dot_nn(ctx2_ref[...], r.cross_out[...]) + r.out_bias[1:2, :].astype(F32)
    )


def attention_kernel(levels, r):
    self_part(
        r, r.x, r.tgt, r.near, r.far, r.q, r.k, r.v, r.ctx, r.lse, r.r1, r.a1, r.work, levels
    )
    bias = r.head_bias[...].astype(F32)
    r.k2[...] = dot_nn(r.memory[...], r.cross_kv[0]).astype(BF16)
    r.v2[...] = (dot_nn(r.memory[...], r.cross_kv[1]) + bias[3:4, :]).astype(BF16)
    cross_part(
        r, r.src, r.near, r.far, r.a1, r.q2, r.k2, r.v2, r.ctx2, r.lse2, r.r2, r.work, levels
    )


def feed_part(r, r2_ref, a2_ref, work_ref, g_ref, slope_ref):
    length = r2_ref.shape[0]
    units = r.ffn_in[0].shape[1]
    chunk = min(256, units)
    gain, shift = r.gain[1:2, :].astype(F32), r.shift[1:2, :].astype(F32)

    def step(tile):
        rows = tile_rows(tile)
        normed = norm_stats(r2_ref[rows, :])[0] * gain + shift
        work_ref[rows, :] = normed
        a2_ref[rows, :] = normed.astype(BF16)

    each_tile(length // TILE, step)
    spots = [(j, first) for j in range(len(r.ffn_in)) for first in range(0, units, chunk)]

    def product(spot):
        j, first = spot
        cut = slice(first, first + chunk)
        return dot_nn(a2_ref[...], r.ffn_in[j][:, cut]) + r.ffn_bias[j][:, cut].astype(F32)

    following = product(spots[0])
    for index, (j, first) in enumerate(spots):
        pre = following
        if index + 1 < len(spots):
            following = product(spots[index + 1])
        phi, bell = gelu_parts(pre)
        cut = slice(j * units + first, j * units + first + chunk)
        g_ref[:, cut] = (pre * phi).astype(BF16)
        if slope_ref is not None:
            slope_ref[:, cut] = (phi + (pre * bell) * 0.3989422804014327).astype(BF16)
    fed = r.out_bias[2:3, :].astype(F32)
    for j in range(len(r.ffn_out)):
        fed = fed + dot_nn(g_ref[:, j * units : (j + 1) * units], r.ffn_out[j][...])
    work_ref[...] += fed


def add_grad(total_ref, left, right):
    total_ref[...] += dot_nn(left, right)


def start_totals(refs):
    @pl.when(pl.program_id(0) == 0)
    def clear():
        for ref in refs:
            ref[...] = jnp.zeros_like(ref)


def end_totals(pairs):
    @pl.when(pl.program_id(0) == pl.num_programs(0) - 1)
    def write():
        for total_ref, out_ref in pairs:
            share = out_ref.shape[2]
            for j in range(out_ref.shape[0]):
                out_ref[j] = total_ref[:, j * share : (j + 1) * share].astype(BF16)


def column_total(values):
    return jnp.sum(values.astype(F32), axis=0, keepdims=True)


def add_share(share_ref, row, values):
    share = share_ref.shape[2]
    for j in range(share_ref.shape[0]):
        share_ref[j, row : row + 1, :] += values[:, j * share : (j + 1) * share]


def feed_kernel(levels, r):
    length = r.r2.shape[0]
    units = r.ffn_in[0].shape[1]
    chunk = min(256, units)
    start_totals([r.in_total, r.out_total, r.common, r.shares])
    feed_part(r, r.r2, r.a2, r.work, r.g, r.slope)
    gain, shift = r.gain[...].astype(F32), r.shift[...].astype(F32)

    def last_norm(tile):
        rows = tile_rows(tile)
        normed, inverse = norm_stats(r.work[rows, :])
        r.second[rows, :] = (normed * gain[2:3, :] + shift[2:3, :]).astype(BF16)
        grad, gain_part, shift_part = norm_back(
            normed, inverse, gain[2:3, :], r.cot[rows, :].astype(F32)
        )
        r.work[rows, :] = grad
        low = grad.astype(BF16)
        r.df[rows, :] = low
        r.common[2:3, :] += column_total(low)
        r.common[5:6, :] += gain_part
        r.common[8:9, :] += shift_part

    each_tile(length // TILE, last_norm)
    spots = [(j, first) for j in range(len(r.ffn_in)) for first in range(0, units, chunk)]

    def product(spot):
        j, first = spot
        return dot_nt(r.df[...], r.ffn_out[j][first : first + chunk, :])

    share = r.shares.shape[2]
    following = product(spots[0])
    for index, (j, first) in enumerate(spots):
        hidden_grad = following.astype(BF16)
        if index + 1 < len(spots):
            following = product(spots[index + 1])
        cut = slice(j * units + first, j * units + first + chunk)
        pre_grad = (hidden_grad.astype(F32) * r.slope[:, cut].astype(F32)).astype(BF16)
        r.du[:, cut] = pre_grad
        sums = column_total(pre_grad)
        for piece in range(0, chunk, share):
            row = 4 + (first + piece) // share
            r.shares[j, row : row + 1, :] += sums[:, piece : piece + share]
    back = r.work[...]
    for j in range(len(r.ffn_in)):
        back = back + dot_nt(r.du[:, j * units : (j + 1) * units], r.ffn_in[j][...])
    r.work[...] = back

    def middle_norm(tile):
        rows = tile_rows(tile)
        normed, inverse = norm_stats(r.r2[rows, :])
        grad, gain_part, shift_part = norm_back(normed, inverse, gain[1:2, :], r.work[rows, :])
        r.dr2[rows, :] = grad
        low = grad.astype(BF16)
        r.common[1:2, :] += column_total(low)
        r.common[4:5, :] += gain_part
        r.common[7:8, :] += shift_part

    each_tile(length // TILE, middle_norm)
    turned = r.a2[...].T
    hidden = r.du.shape[1]
    wide = min(512, hidden)
    for first in range(0, hidden, wide):
        cut = slice(first, first + wide)
        r.in_total[:, cut] += dot_nn(turned, r.du[:, cut])
    turned = r.df[...].T
    for first in range(0, hidden, wide):
        cut = slice(first, first + wide)
        r.out_total[:, cut] += dot_nn(turned, r.g[:, cut])
    end_totals([(r.in_total, r.ffn_in_grad), (r.out_total, r.ffn_out_grad)])


def cross_back_kernel(levels, r):
    tiles, width = r.dr2.shape[0] // TILE, r.dr2.shape[1]
    start_totals([r.total_q, r.total_k, r.total_v, r.total_o, r.common, r.shares])
    far, unused = make_marks(r.tgt[...], levels, width // HEAD_DIM)
    unused, near = make_marks(r.src[...], levels, width // HEAD_DIM)
    r.far[...] = far
    r.near[...] = near
    r.low[...] = r.dr2[...].astype(BF16)
    r.dctx[...] = dot_nt(r.low[...], r.cross_out[...]).astype(BF16)
    base = (pl.num_programs(0) + pl.program_id(0)) * tiles
    attend_back(
        r.q2,
        r.k2,
        r.v2,
        r.far,
        r.near,
        r.sides,
        r.own,
        r.spread,
        r.lse2,
        r.ctx2,
        r.dctx,
        r.dq,
        r.dk,
        r.dv,
        r.starts,
        base,
    )
    r.dk_low[...] = r.dk[...].astype(BF16)
    r.dv_low[...] = r.dv[...].astype(BF16)
    r.memory_grad[...] = (
        dot_nt(r.dk_low[...], r.cross_kv[0]) + dot_nt(r.dv_low[...], r.cross_kv[1])
    ).astype(BF16)
    r.work[...] = r.dr2[...] + dot_nt(r.dq[...], r.cross_q[...])
    add_grad(r.total_o, r.low[...].T, r.ctx2[...])
    turned = r.memory[...].T
    add_grad(r.total_k, turned, r.dk_low[...])
    add_grad(r.total_v, turned, r.dv_low[...])
    add_grad(r.total_q, r.a1[...].T, r.dq[...])
    add_share(r.shares, 2, column_total(r.dq[...]))
    add_share(r.shares, 3, column_total(r.dv_low[...]))
    gain = r.gain[0:1, :].astype(F32)

    def first_norm(tile):
        rows = tile_rows(tile)
        normed, inverse = norm_stats(r.r1[rows, :])
        grad, gain_part, shift_part = norm_back(normed, inverse, gain, r.work[rows, :])
        r.dr1[rows, :] = grad
        r.common[0:1, :] += column_total(grad.astype(BF16))
        r.common[3:4, :] += gain_part
        r.common[6:7, :] += shift_part

    each_tile(tiles, first_norm)
    end_totals(
        [
            (r.total_q, r.cross_q_grad),
            (r.total_k, r.cross_k_grad),
            (r.total_v, r.cross_v_grad),
            (r.total_o, r.cross_out_grad),
        ]
    )


def self_back_kernel(levels, r):
    tiles, width = r.dr1.shape[0] // TILE, r.dr1.shape[1]
    start_totals([r.total_q, r.total_k, r.total_v, r.total_o, r.shares])
    far, near = make_marks(r.tgt[...], levels, width // HEAD_DIM)
    r.far[...] = far
    r.near[...] = near
    r.low[...] = r.dr1[...].astype(BF16)
    r.dctx[...] = dot_nt(r.low[...], r.self_out[...]).astype(BF16)
    attend_back(
        r.q,
        r.k,
        r.v,
        r.far,
        r.near,
        r.sides,
        r.own,
        r.spread,
        r.lse,
        r.ctx,
        r.dctx,
        r.dq,
        r.dk,
        r.dv,
        r.starts,
        pl.program_id(0) * tiles,
    )
    r.dk_low[...] = r.dk[...].astype(BF16)
    r.dv_low[...] = r.dv[...].astype(BF16)
    r.input_grad[...] = (
        r.dr1[...]
        + (dot_nt(r.dq[...], r.self_qkv[0]) + dot_nt(r.dk_low[...], r.self_qkv[1]))
        + dot_nt(r.dv_low[...], r.self_qkv[2])
    ).astype(BF16)
    add_grad(r.total_o, r.low[...].T, r.ctx[...])
    turned = r.x[...].T
    add_grad(r.total_q, turned, r.dq[...])
    add_grad(r.total_k, turned, r.dk_low[...])
    add_grad(r.total_v, turned, r.dv_low[...])
    add_share(r.shares, 0, column_total(r.dq[...]))
    add_share(r.shares, 1, column_total(r.dv_low[...]))
    end_totals(
        [
            (r.total_q, r.self_q_grad),
            (r.total_k, r.self_k_grad),
            (r.total_v, r.self_v_grad),
            (r.total_o, r.self_out_grad),
        ]
    )


def first_pass_kernel(levels, r):
    tiles = r.x.shape[0] // TILE
    self_part(
        r, r.x, r.tgt, r.near, r.far, r.q, r.k, r.v, r.ctx, None, None, r.low, r.work, levels
    )
    cross_part(
        r, r.src, r.near, r.far, r.low, r.q, r.k2, r.v2, r.ctx, None, r.r2, r.work, levels
    )
    feed_part(r, r.r2, r.low, r.work, r.g, None)
    gain, shift = r.gain[2:3, :].astype(F32), r.shift[2:3, :].astype(F32)

    def last_norm(tile):
        rows = tile_rows(tile)
        r.first[rows, :] = (norm_stats(r.work[rows, :])[0] * gain + shift).astype(BF16)

    each_tile(tiles, last_norm)


class Refs:
    pass


def call_rows(kernel, name, rows, levels, scalars, row_args, fixed_args, row_outs, fixed_outs, scratch):
    names, args, specs = [], [], []

    def put(key, array, fixed):
        zeros = (0,) * (array.ndim if fixed else array.ndim - 1)
        names.append(key)
        args.append(array)
        if fixed:
            specs.append(
                pl.BlockSpec(array.shape, lambda row, *_: zeros, pipeline_mode=pl.Buffered(1))
            )
        else:
            specs.append(
                pl.BlockSpec((None,) + array.shape[1:], lambda row, *_: (row,) + zeros)
            )

    for group, fixed in ((row_args, False), (fixed_args, True)):
        for key, value in group.items():
            if isinstance(value, tuple):
                for index, array in enumerate(value):
                    put((key, index), array, fixed)
            else:
                put(key, value, fixed)
    out_names, out_shapes, out_specs = [], [], []
    for key, (shape, kind) in row_outs.items():
        tail = (0,) * (len(shape) - 1)
        out_names.append(key)
        out_shapes.append(jax.ShapeDtypeStruct(shape, kind))
        out_specs.append(
            pl.BlockSpec((None,) + shape[1:], lambda row, *_, tail=tail: (row,) + tail)
        )
    for key, (shape, kind) in fixed_outs.items():
        zeros = (0,) * len(shape)
        out_names.append(key)
        out_shapes.append(jax.ShapeDtypeStruct(shape, kind))
        out_specs.append(pl.BlockSpec(shape, lambda row, *_, zeros=zeros: zeros))
    all_names = list(scalars) + names + out_names + list(scratch)

    def run(*refs):
        found = Refs()
        for key, ref in zip(all_names, refs):
            if isinstance(key, tuple):
                if key[1] == 0:
                    setattr(found, key[0], [])
                getattr(found, key[0]).append(ref)
            else:
                setattr(found, key, ref)
        kernel(levels, found)

    outs = pl.pallas_call(
        run,
        grid_spec=pltpu.PrefetchScalarGridSpec(
            num_scalar_prefetch=len(scalars),
            grid=(rows,),
            in_specs=specs,
            out_specs=tuple(out_specs),
            scratch_shapes=[pltpu.VMEM(shape, kind) for shape, kind in scratch.values()],
        ),
        out_shape=tuple(out_shapes),
        compiler_params=pltpu.CompilerParams(
            dimension_semantics=("arbitrary",), vmem_limit_bytes=VMEM_BYTES
        ),
        cost_estimate=pl.CostEstimate(flops=1000, bytes_accessed=1000, transcendentals=0),
        name=name,
    )(*scalars.values(), *args)
    return dict(zip(out_names, outs))


def from_peer(values, size, step):
    return lax.ppermute(values, "head", [((i + step) % size, i) for i in range(size)])


def by_origin(parts, me):
    count = len(parts)
    if count == 1:
        return parts
    if count == 2:
        return [
            jnp.where(me == 0, parts[0], parts[1]),
            jnp.where(me == 0, parts[1], parts[0]),
        ]
    stacked = jnp.stack(parts)
    return [
        lax.dynamic_index_in_dim(stacked, (origin - me) % count, 0, keepdims=False)
        for origin in range(count)
    ]


def own_first(values, size):
    return tuple([values] + [from_peer(values, size, step) for step in range(1, size)])


def trade_parts(values, split_axis, join_axis, me, size):
    share = values.shape[split_axis] // size
    parts = []
    for step in range(size):
        target = (me - step) % size
        part = lax.dynamic_slice_in_dim(values, target * share, share, split_axis)
        parts.append(part if step == 0 else from_peer(part, size, step))
    return jnp.concatenate(by_origin(parts, me), axis=join_axis)


def head_share(parts, size):
    total = parts[0].astype(F32)
    for step in range(1, size):
        arrived = lax.ppermute(parts[step], "head", [(i, (i + step) % size) for i in range(size)])
        total = total + arrived.astype(F32)
    return total.astype(BF16)


def stage_orders(dp_size):
    bits = [1 << b for b in range(dp_size.bit_length() - 1)]
    return bits, bits[:2][::-1] + bits[2:]


def reduce_kernel(dp_size, head_size, count, *refs):
    grads = refs[:count]
    common_one, common_two, share_one, share_two, share_three = refs[count : count + 5]
    out_ref, small_out_ref = refs[count + 5 : count + 7]
    head_land, land, small_land, small_ref, sum_ref = refs[count + 7 : count + 12]
    (
        local_sem,
        head_send,
        head_recv,
        fold_send,
        fold_recv,
        grow_send,
        grow_recv,
        small_send,
        small_recv,
    ) = refs[count + 12 :]
    length = out_ref.shape[1]
    me, spot = lax.axis_index("head"), lax.axis_index("dp")
    orders = stage_orders(dp_size)
    depth = len(orders[0])

    def digit(stride):
        return (spot // stride) % 2

    def partner(stride):
        return spot + (1 - 2 * digit(stride)) * stride

    share = out_ref.shape[2]
    for j in range(head_size):
        small_ref[j, 0:16, :] = common_one[...] + common_two[...]
        small_ref[j, 16:24, 0:share] = share_one[j] + share_two[j] + share_three[j]
        if share < small_ref.shape[2]:
            small_ref[j, 16:24, share:] = jnp.zeros((8, small_ref.shape[2] - share), F32)
    peers = [(me + step) % head_size for step in range(1, head_size)]
    barrier = pltpu.get_barrier_semaphore()
    for peer in peers:
        pl.semaphore_signal(
            barrier, inc=1, device_id={"head": peer}, device_id_type=pl.DeviceIdType.MESH
        )
    for stride in orders[0]:
        pl.semaphore_signal(
            barrier, inc=1, device_id={"dp": partner(stride)}, device_id_type=pl.DeviceIdType.MESH
        )
    pl.semaphore_wait(barrier, len(peers) + depth)

    def remote(source, target, send, recv, where):
        return pltpu.make_async_remote_copy(
            src_ref=source,
            dst_ref=target,
            send_sem=send,
            recv_sem=recv,
            device_id=where,
            device_id_type=pl.DeviceIdType.MESH,
        )

    queue = [i for pair in zip(range(count // 2), range(count // 2, count)) for i in pair]
    small_head = [
        remote(
            small_ref.at[j + 1],
            small_land.at[j],
            small_send.at[j],
            small_recv.at[j],
            {"head": peer},
        )
        for j, peer in enumerate(peers)
    ]
    for copy in small_head:
        copy.start()
    locals_, heads_ = {}, {}
    for i in queue:
        locals_[i] = pltpu.make_async_copy(grads[i].at[0], sum_ref.at[i], local_sem.at[i])
        locals_[i].start()
        heads_[i] = [
            remote(
                grads[i].at[j + 1],
                head_land.at[j, i],
                head_send.at[j, i],
                head_recv.at[j, i],
                {"head": peer},
            )
            for j, peer in enumerate(peers)
        ]
        for copy in heads_[i]:
            copy.start()

    def places(i):
        order = orders[0] if i < count // 2 else orders[1]
        offset, size, result = 0, length, []
        for stride in order:
            size //= 2
            keep = offset + digit(stride) * size
            give = offset + (1 - digit(stride)) * size
            result.append((stride, size, pl.multiple_of(keep, 16), pl.multiple_of(give, 16)))
            offset = keep
        return result

    plan = {i: places(i) for i in range(count)}
    moving = {}

    def fold(i, stage):
        stride, size, keep, give = plan[i][stage]
        base = length - (length >> stage)
        copy = remote(
            sum_ref.at[i, pl.ds(give, size), :],
            land.at[i, pl.ds(base, size), :],
            fold_send.at[stage, i],
            fold_recv.at[stage, i],
            {"dp": partner(stride)},
        )
        copy.start()
        moving[i] = copy

    def grow(i, stage):
        stride, size, keep, give = plan[i][stage]
        rows = out_ref.at[i, pl.ds(keep, size), :]
        copy = remote(
            rows, rows, grow_send.at[stage, i], grow_recv.at[stage, i], {"dp": partner(stride)}
        )
        copy.start()
        moving[i] = copy

    def task(i, number):
        if number == 0:
            locals_[i].wait()
            total = sum_ref[i].astype(F32)
            for j, copy in enumerate(heads_[i]):
                copy.wait()
                total = total + head_land[j, i].astype(F32)
            sum_ref[i] = total.astype(BF16)
            fold(i, 0)
        elif number <= depth:
            moving[i].wait()
            stage = number - 1
            stride, size, keep, give = plan[i][stage]
            base = length - (length >> stage)
            rows = pl.ds(keep, size)
            total = (
                sum_ref[i, rows, :].astype(F32) + land[i, pl.ds(base, size), :].astype(F32)
            ).astype(BF16)
            if number < depth:
                sum_ref[i, rows, :] = total
                fold(i, number)
            else:
                out_ref[i, rows, :] = total
                grow(i, depth - 1)
        else:
            moving[i].wait()
            stage = 2 * depth - number
            if stage > 0:
                grow(i, stage - 1)

    steps = 2 * depth + 1
    small_moving = None
    for time in range(steps + count // 2 - 1):
        if time == 0:
            total = small_ref[0]
            for j, copy in enumerate(small_head):
                copy.wait()
                total = total + small_land[j]
            small_out_ref[...] = total
        elif time <= depth:
            small_moving.wait()
            small_out_ref[...] += small_land[len(peers) + time - 1]
        if time < depth:
            slot = len(peers) + time
            small_moving = remote(
                small_out_ref,
                small_land.at[slot],
                small_send.at[slot],
                small_recv.at[slot],
                {"dp": partner(orders[0][time])},
            )
            small_moving.start()
        for place, i in enumerate(queue):
            number = time - place // 2
            if 0 <= number < steps:
                task(i, number)


def reduce_grads(grads, common, shares, dp_size, head_size):
    count = len(grads)
    length, share = grads[0].shape[1:]
    depth = dp_size.bit_length() - 1
    peers = head_size - 1
    small = (24, common[0].shape[1])
    any_spec = pl.BlockSpec(memory_space=pl.ANY)
    vmem = pl.BlockSpec(memory_space=pltpu.VMEM)
    dma = pltpu.SemaphoreType.DMA
    return pl.pallas_call(
        functools.partial(reduce_kernel, dp_size, head_size, count),
        out_shape=(
            jax.ShapeDtypeStruct((count, length, share), BF16),
            jax.ShapeDtypeStruct(small, F32),
        ),
        in_specs=[any_spec] * count + [vmem] * 5,
        out_specs=(vmem, vmem),
        scratch_shapes=[
            pltpu.VMEM((peers, count, length, share), BF16),
            pltpu.VMEM((count, length, share), BF16),
            pltpu.VMEM((peers + depth,) + small, F32),
            pltpu.VMEM((head_size,) + small, F32),
            pltpu.VMEM((count, length, share), BF16),
            dma((count,)),
            dma((peers, count)),
            dma((peers, count)),
            dma((depth, count)),
            dma((depth, count)),
            dma((depth, count)),
            dma((depth, count)),
            dma((peers + depth,)),
            dma((peers + depth,)),
        ],
        compiler_params=pltpu.CompilerParams(
            collective_id=0, has_side_effects=True, vmem_limit_bytes=VMEM_BYTES
        ),
        name="reduce",
    )(*grads, *common, *shares)


def window_starts(query_segments, key_segments, window):
    rows, length = query_segments.shape
    tiles = query_segments.reshape(rows, length // TILE, TILE)
    first, last = tiles[:, :, 0], tiles[:, :, -1]
    before = jnp.sum(key_segments[:, None, :] < first[:, :, None], axis=2).astype(jnp.int32)
    after = jnp.sum(key_segments[:, None, :] <= last[:, :, None], axis=2).astype(jnp.int32)
    start = jnp.minimum((before // 16) * 16, key_segments.shape[1] - window)
    return jnp.where(after - start <= window, start, -1).reshape(-1)


def constants(width, levels):
    heads = width // HEAD_DIM
    lane = np.arange(PAIR)
    sides = np.stack([lane < HEAD_DIM, lane >= HEAD_DIM])
    kept = (lane >= 16) & (lane < 16 + 3 * heads)
    own = np.stack([(lane < levels) | (kept & ((lane - 16) % heads == h)) for h in range(heads)])
    spread = kept[None, :] & (
        (lane[None, :] - 16) % heads == np.arange(width)[:, None] // HEAD_DIM
    )

    def tall(rows):
        return jnp.asarray(np.broadcast_to(rows[:, None, :], (rows.shape[0], TILE, PAIR)), BF16)

    return {"sides": tall(sides), "own": tall(own), "spread": jnp.asarray(spread, BF16)}


def local_layer(
    source,
    mixed,
    memory,
    cotangent,
    tgt_segments,
    src_segments,
    levels,
    weights,
    head_size=1,
    feed_sums=lambda grads: grads,
):
    rows, length, width = mixed.shape
    hidden = sum(part.shape[1] for part in weights["ffn_in"])
    heads = width // HEAD_DIM
    tiles = length // TILE
    window = min(WINDOW, length)
    share = width // head_size
    marks = constants(width, levels)
    sides = {"sides": marks["sides"]}
    tgt, src = tgt_segments[:, None, :], src_segments[:, None, :]
    starts = {
        "starts": jnp.concatenate(
            [
                window_starts(tgt_segments, tgt_segments, window),
                window_starts(tgt_segments, src_segments, window),
            ]
        )
    }

    def pick(*keys):
        return {key: weights[key] for key in keys}

    wide_low = ((rows, length, width), BF16)
    wide = ((rows, length, width), F32)
    stats = ((rows, tiles, heads, TILE), F32)
    one_low, one = ((length, width), BF16), ((length, width), F32)
    mark = ((length, PAIR), BF16)
    square = ((width, width), F32)
    split = ((head_size, width, share), BF16)
    common, shares = ((16, width), F32), ((head_size, 8, share), F32)
    norms = pick("out_bias", "gain", "shift")
    attention = pick("self_qkv", "self_out", "cross_q", "cross_kv", "cross_out", "head_bias")
    feed = pick("ffn_in", "ffn_out", "ffn_bias")
    kept = call_rows(
        attention_kernel,
        "attention",
        rows,
        levels,
        starts,
        {"x": mixed, "memory": memory, "tgt": tgt, "src": src},
        sides | attention | norms,
        {key: wide_low for key in ("q", "k", "v", "ctx", "a1", "q2", "k2", "v2", "ctx2")}
        | {"lse": stats, "lse2": stats, "r1": wide, "r2": wide},
        {},
        {"work": one, "far": mark, "near": mark},
    )
    fed = call_rows(
        feed_kernel,
        "feed",
        rows,
        levels,
        {},
        {"r2": kept["r2"], "cot": cotangent},
        feed | norms,
        {"second": wide_low, "dr2": wide},
        {
            "ffn_in_grad": ((head_size, width, hidden // head_size), BF16),
            "ffn_out_grad": ((head_size, width, hidden // head_size), BF16),
            "common": common,
            "shares": shares,
        },
        {
            "a2": one_low,
            "df": one_low,
            "work": one,
            "g": ((length, hidden), BF16),
            "du": ((length, hidden), BF16),
            "slope": ((length, hidden), BF16),
            "in_total": ((width, hidden), F32),
            "out_total": ((width, hidden), F32),
        },
    )
    feed_grads = feed_sums((fed["ffn_in_grad"], fed["ffn_out_grad"]))
    dr2, feed_grads = lax.optimization_barrier((fed["dr2"], feed_grads))
    totals = {"total_" + key: square for key in "qkvo"}
    back_scratch = totals | {
        "far": mark,
        "near": mark,
        "dctx": one_low,
        "low": one_low,
        "dq": one_low,
        "dk_low": one_low,
        "dv_low": one_low,
        "dk": one,
        "dv": one,
    }
    crossed = call_rows(
        cross_back_kernel,
        "cross_back",
        rows,
        levels,
        starts,
        {key: kept[key] for key in ("q2", "k2", "v2", "ctx2", "lse2", "r1", "a1")}
        | {"dr2": dr2, "memory": memory, "tgt": tgt, "src": src},
        marks | pick("cross_q", "cross_kv", "cross_out", "gain"),
        {"memory_grad": wide_low, "dr1": wide},
        {key: split for key in ("cross_q_grad", "cross_k_grad", "cross_v_grad", "cross_out_grad")}
        | {"common": common, "shares": shares},
        back_scratch | {"work": one},
    )
    selfed = call_rows(
        self_back_kernel,
        "self_back",
        rows,
        levels,
        starts,
        {key: kept[key] for key in ("q", "k", "v", "ctx", "lse")}
        | {"dr1": crossed["dr1"], "x": mixed, "tgt": tgt},
        marks | pick("self_qkv", "self_out"),
        {"input_grad": wide_low},
        {key: split for key in ("self_q_grad", "self_k_grad", "self_v_grad", "self_out_grad")}
        | {"shares": shares},
        back_scratch,
    )
    source, input_grad = lax.optimization_barrier((source, selfed["input_grad"]))
    first = call_rows(
        first_pass_kernel,
        "first_pass",
        rows,
        levels,
        starts,
        {"x": source, "k2": kept["k2"], "v2": kept["v2"], "tgt": tgt, "src": src},
        sides
        | pick("self_qkv", "self_out", "cross_q", "cross_out", "head_bias")
        | feed
        | norms,
        {"first": wide_low},
        {},
        {
            "q": one_low,
            "k": one_low,
            "v": one_low,
            "ctx": one_low,
            "low": one_low,
            "r2": one,
            "work": one,
            "g": ((length, hidden), BF16),
            "far": mark,
            "near": mark,
        },
    )
    grads = tuple(
        crossed[key] for key in ("cross_q_grad", "cross_k_grad", "cross_v_grad", "cross_out_grad")
    ) + tuple(selfed[key] for key in ("self_q_grad", "self_k_grad", "self_v_grad", "self_out_grad"))
    return (
        first["first"],
        fed["second"],
        input_grad,
        crossed["memory_grad"],
        feed_grads,
        grads,
        (fed["common"], crossed["common"]),
        (fed["shares"], crossed["shares"], selfed["shares"]),
    )


def body(
    dp_size,
    head_size,
    source_copy,
    target_embed,
    memory,
    tgt_segments,
    src_segments,
    hamming,
    priority,
    cotangent,
    self_qkv,
    self_out,
    cross_q,
    cross_kv,
    cross_out,
    ffn_in,
    ffn_out,
    head_bias,
    ffn_bias,
    out_bias,
    norm_gain,
    norm_shift,
):
    me = lax.axis_index("head")
    levels = hamming.shape[1]
    held, share, width = source_copy.shape
    rows = held // head_size

    def own_positions(array):
        return lax.dynamic_slice_in_dim(array, me * share, share, 1)

    def own_rows(array):
        return lax.dynamic_slice_in_dim(array, me * rows, rows, 0)

    level = jnp.arange(levels, dtype=jnp.int32)
    chosen = own_positions(tgt_segments)[:, :, None] == level[None, None, :]
    limits = jnp.sum(jnp.where(chosen, hamming[:, None, :], 0), axis=2)
    glanced = own_positions(priority) < limits
    mixed_part = jnp.where(glanced[:, :, None], target_embed, source_copy)

    def gather(values, axis):
        return jnp.concatenate(own_first(values, head_size), axis=axis)

    trade = functools.partial(trade_parts, me=me, size=head_size)
    (
        first_out,
        second_out,
        input_grad,
        memory_grad,
        feed_grads,
        grads,
        common,
        shares,
    ) = local_layer(
        trade(source_copy, 0, 1),
        trade(mixed_part, 0, 1),
        trade(memory, 0, 1),
        trade(cotangent, 0, 1),
        own_rows(tgt_segments),
        own_rows(src_segments),
        levels,
        {
            "self_qkv": gather(self_qkv, 2),
            "self_out": gather(self_out, 0),
            "cross_q": gather(cross_q, 1),
            "cross_kv": gather(cross_kv, 2),
            "cross_out": gather(cross_out, 0),
            "head_bias": gather(head_bias, 1),
            "ffn_bias": own_first(ffn_bias[None, :], head_size),
            "ffn_in": own_first(ffn_in, head_size),
            "ffn_out": own_first(ffn_out, head_size),
            "out_bias": out_bias,
            "gain": norm_gain,
            "shift": norm_shift,
        },
        head_size,
        lambda pair: tuple(head_share(parts, head_size) for parts in pair),
    )
    ffn_in_grad, ffn_out_grad = lax.psum(feed_grads, "dp")
    first_out, ffn_in_grad, ffn_out_grad = lax.optimization_barrier(
        (first_out, ffn_in_grad, ffn_out_grad)
    )
    common = lax.optimization_barrier((common, first_out))[0]
    summed, sums = reduce_grads(grads, common, shares, dp_size, head_size)
    summed = summed.astype(F32)
    part = width // head_size

    def back(array):
        return trade(array, 1, 0)

    return (
        back(first_out),
        back(second_out),
        back(input_grad),
        back(memory_grad),
        summed[4:7],
        summed[7].T,
        summed[0],
        summed[1:3],
        summed[3].T,
        ffn_in_grad.astype(F32),
        ffn_out_grad.T.astype(F32),
        sums[16:20, :part],
        sums[20:24, :part].reshape(-1),
        sums[0:3],
        sums[3:6],
        sums[6:9],
    )


def solution(mesh):
    split = P("dp", "head", None)
    rows = P("dp", None)
    last, last_two, first = P(None, "head"), P(None, None, "head"), P("head", None)
    return jax.shard_map(
        functools.partial(body, mesh.shape["dp"], mesh.shape["head"]),
        mesh=mesh,
        in_specs=(split, split, split, rows, rows, rows, rows, split)
        + (last_two, first, last, last_two, first, last, first, last, P("head"), P(), P(), P()),
        out_specs=(split, split, split, split)
        + (last_two, first, last, last_two, first, last, first, last, P("head"), P(), P(), P()),
        check_vma=False,
    )
```

time: 1340 us -> 416 us (0.31)
  matrix products: 481 us -> 0 us
  Pallas kernels: 0 us -> 303 us
  local copies, waits for them, and re-layouts: 312 us -> 46.6 us
  waiting for transfers between devices: 234 us -> 0.07 us
  other arithmetic: 194 us -> 39.6 us
  blocking collectives: 83.6 us -> 0 us
    dot_general x182 -> x0, matrix products: 481 us -> none  [the longest x18 141 us: project(): return jnp.dot(left, right, preferred_element_type=jnp.float32)]
    pallas_call x0 -> x6, Pallas kernels: none -> 303 us  [the longest x5 239 us: call_rows(): pl.pallas_call(run, grid_spec=pltpu.PrefetchScalarGridSpec(num_scalar_pre...]
    dynamic_slice x224 -> x11, local copies, waits for them, and re-layouts: 180 us -> 14.7 us  [the longest x8 14.6 us: trade_parts(): part = lax.dynamic_slice_in_dim(values, target * share, share, split_axis)]
    reduce_sum x53 -> x2, other arithmetic: 93.7 us -> 1.21 us  [the longest x1 0.78 us: body(): limits = jnp.sum(jnp.where(chosen, hamming[:, None, :], 0), axis=2)]
    all_gather x10 -> x0, waiting for transfers between devices: 86.9 us -> none  [the longest x7 50.5 us: gather_share(): return lax.all_gather(shares, 'head', axis=1, tiled=True)]
    psum x2 -> x0, blocking collectives: 83.6 us -> none  [the longest x1 43.2 us: body(): lax.psum((out_bias_part, gain_part, shift_part), ('dp', 'head'))]
    reduce_scatter x10 -> x0, waiting for transfers between devices: 77.6 us -> none  [the longest x6 37.1 us: branch_total(): lax.psum_scatter(partial_value.astype(jnp.bfloat16), 'head', scatter_dime...]
    convert_element_type x30 -> x5, other arithmetic: 83.4 us -> 11.8 us  [the longest x2 5.36 us: head_share(): return total.astype(BF16)]
  transfers between devices with their start and end apart: 21 -> 20, of which waited for: 15 -> 0; matrix products, arithmetic and copies ran while one was open for 31% -> 17% of each run, Pallas kernels for 0% -> 59%
where the time goes in v2:
time: 416 us; the launch traced here: 410 us
  Pallas kernels  303 us (73%)
  local copies, waits for them, and re-layouts  46.6 us (11%)
  other arithmetic  39.6 us (10%)
  between operations  14.8 us (4%)
  starting transfers between devices  6.36 us (2%)
    pallas_call x5, Pallas kernels, call_rows(): pl.pallas_call(run, grid_spec=pltpu.PrefetchScalarGridSpec(num_scalar_pre...  239 us
    pallas_call x1, Pallas kernels, reduce_grads(): pl.pallas_call(functools.partial(reduce_kernel, dp_size, head_size, count...  64.2 us
    unnamed x67, local copies, waits for them, and re-layouts  16.8 us
    dynamic_slice x8, local copies, waits for them, and re-layouts, trade_parts(): part = lax.dynamic_slice_in_dim(values, target * share, share, split_axis)  14.6 us
    concatenate x7, other arithmetic, trade_parts(): return jnp.concatenate(by_origin(parts, me), axis=join_axis)  11.5 us
    select_n x8, other arithmetic, by_origin(): jnp.where(me == 0, parts[0], parts[1])  11.3 us
  transfers between devices with their start and end apart: 20, of which 0 were waited for; matrix products, arithmetic and copies ran while one was open for 17% of the time, Pallas kernels for 59%

profile of v2, /device:TPU:0, one launch (start us, length us, event | category | flops | bytes accessed | tf_op | source)
XLA Modules:
  0.0 410.1 jit_solution(8037434750156566109)
XLA Ops:
  7.3 0.6 copy-done
  7.9 0.8 select_reduce_fusion
  8.7 0.7 dynamic-slice_compare_fusion
  9.4 2.4 broadcast_select_fusion
  11.8 1.3 copy-done.6
  13.2 1.0 constant_dynamic-slice_fusion.6
  15.7 1.2 constant_dynamic-update-slice_fusion.1
  16.9 2.3 constant_dynamic-slice_fusion.5
  20.2 1.1 constant_dynamic-update-slice_fusion.7
  21.3 2.3 constant_dynamic-slice_fusion.4
  23.6 1.7 constant_dynamic-update-slice_fusion.5
  25.3 1.7 constant_dynamic-update-slice_fusion.9
  27.5 0.6 pad_add_fusion.refs_0_
  28.1 0.6 broadcast_in_dim.43.refs_3_.refs_10_.refs_8_.refs_4_
  28.7 0.6 broadcast_in_dim.44.refs_4_.refs_11_.refs_5_
  29.5 1.1 constant_dynamic-update-slice_fusion.2.refs_7_.refs_13_.refs_8_
  30.6 1.9 constant_dynamic-update-slice_fusion.4.refs_8_.refs_15_.refs_9_
  32.9 0.7 constant_dynamic-update-slice_fusion.8.refs_10_.refs_17_
  33.8 1.1 constant_dynamic-update-slice_fusion.6.refs_9_.refs_16_
  35.3 1.2 constant_dynamic-update-slice_fusion.refs_6_.refs_12_.refs_7_
  37.0 2.1 broadcast_select_fusion.14
  39.2 1.4 broadcast_select_fusion.12
  40.5 2.5 pad_maximum_fusion.1
  43.2 1.6 pad_maximum_fusion.3.refs_1_
  44.7 43.6 %attention.1 = (bf16[4,512,512]{2,1,0:T(8,128)(2,1)}, bf16[4,512,512]{2,1,0:T(8,128)(2,1)}, bf16[4,512,512]{2,1,0:T(8,128)(2,1)}, bf16[4,512,512]{2,1,0:T(8,128)...) custom-call(s32[32]{0:T(128)} %pad_add_fusion.refs_0_, ...), custom_call_target="tpu_custom_call" | custom-call | flops 1000 | bytes 1000 | tf_op jit(solution)/shard_map/attention/pallas_call | solution.py:638
  88.4 0.6 copy-done.24
  89.0 60.3 %feed.1 = (bf16[4,512,512]{2,1,0:T(8,128)(2,1)}, f32[4,512,512]{2,1,0:T(8,128)}, bf16[2,512,1024]{2,1,0:T(8,128)(2,1)}, bf16[2,512,1024]{2,1,0:T(8,128)(2,1)}, f32[16,512]{1,0:T(8,128)}, /*index=5*/f32[2,8,256]{2,1,0:T(8,128)}) custom-call(f32[4,512,512]{2,1,0:T(8,128)} %get-tuple-element.73.refs_0_, bf16[4,512,512]{2,1,0:T(8,128)(2,1)} %pad_maximum_fusion.3.refs_1_, ...), custom_call_target="tpu_custom_call" | custom-call | flops 1000 | bytes 1000 | tf_op jit(solution)/shard_map/feed/pallas_call | solution.py:638
  149.3 2.4 slice_bitcast_fusion
  151.9 1.1 slice_bitcast_fusion.1
  153.3 1.0 constant_dynamic-slice_fusion.8
  154.5 2.4 constant_dynamic-slice_fusion.2
  157.3 2.8 fusion
  160.0 2.6 fusion.1
  162.7 40.9 %cross_back.1 = (bf16[4,512,512]{2,1,0:T(8,128)(2,1)}, f32[4,512,512]{2,1,0:T(8,128)}, bf16[2,512,256]{2,1,0:T(8,128)(2,1)}, bf16[2,512,256]{2,1,0:T(8,128)(2,1)...) custom-call(s32[32]{0:T(128)} %pad_add_fusion.refs_0_, ...), custom_call_target="tpu_custom_call" | custom-call | flops 1000 | bytes 1000 | tf_op jit(solution)/shard_map/cross_back/pallas_call | solution.py:638
  203.6 2.3 constant_dynamic-slice_fusion
  205.9 1.4 broadcast_select_fusion.16
  207.3 1.5 pad_maximum_fusion.refs_1_
  208.8 30.3 %self_back.1 = (bf16[4,512,512]{2,1,0:T(8,128)(2,1)}, bf16[2,512,256]{2,1,0:T(8,128)(2,1)}, bf16[2,512,256]{2,1,0:T(8,128)(2,1)}, bf16[2,512,256]{2,1,0:T(8,128)...) custom-call(s32[32]{0:T(128)} %pad_add_fusion.refs_0_, bf16[4,512,512]{2,1,0:T(8,128)(2,1)} %get-tuple-element.61.refs_1_, ...), custom_call_target="tpu_custom_call" | custom-call | flops 1000 | bytes 1000 | tf_op jit(solution)/shard_map/self_back/pallas_call | solution.py:638
  239.1 2.3 constant_dynamic-slice_fusion.1
  241.3 1.8 collective-permute-start.17
  243.1 63.4 %first_pass.1 = bf16[4,512,512]{2,1,0:T(8,128)(2,1)} custom-call(s32[32]{0:T(128)} %pad_add_fusion.refs_0_, bf16[4,512,512]{2,1,0:T(8,128)(2,1)} %pad_maximum_fusion.refs_1_, bf16[4,512,512]{2,1,0:T(8,128)(2,1)} %get-tuple-element.67.refs_2_, bf16[4,512,512]{2,1,0:T(8,128)(2,1)} %get-tuple-element.68.refs_3_, ...), custom_call_target="tpu_custom_call" | custom-call | flops 1000 | bytes 1000 | tf_op jit(solution)/shard_map/first_pass/pallas_call | solution.py:638
  307.0 1.5 pad_maximum_fusion.5
  308.5 0.8 copy-done.14
  309.4 1.6 broadcast_select_fusion.2
  311.0 1.5 pad_maximum_fusion.7
  312.5 0.8 copy-done.15
  313.4 2.6 broadcast_select_fusion.4
  316.0 1.0 constant_dynamic-slice_fusion.3
  317.6 1.5 pad_maximum_fusion.6
  319.1 64.2 %reduce.5 = (bf16[8,512,256]{2,1,0:T(8,128)(2,1)}, f32[24,512]{1,0:T(8,128)}) custom-call(bf16[2,512,256]{2,1,0:T(8,128)(2,1)} %get-tuple-element.87.refs_0_, bf16[2,512,256]{2,1,0:T(8,128)(2,1)} %get-tuple-element.88.refs_1_, bf16[2,512,256]{2,1,0:T(8,128)(2,1)} %get-tuple-element.89.refs_2_, bf16[2,512,256]{2,1,0:T(8,128)(2,1)} %get-tuple-element.90.refs_3_, ...), custom_call_target="tpu_custom_call" | custom-call | tf_op jit(solution)/shard_map/reduce/pallas_call | solution.py:892
  383.3 2.1 convert_element_type.60
  385.5 1.3 slice.68
  386.8 1.0 slice.71
  387.9 0.9 slice_bitcast_fusion.2
  388.8 1.0 copy.48
  389.8 1.0 copy.49
  390.8 0.6 slice_bitcast_fusion.5
  391.4 0.6 copy.51
  392.0 2.8 convert_bitcast_fusion
  394.8 3.0 copy.50
  397.7 1.6 convert_element_type.61
  399.3 0.6 fusion.2
  399.9 1.6 broadcast_select_fusion.8
  401.5 1.5 pad_maximum_fusion.4
  (108 shorter events, 7.1 us)
Async XLA Ops:
  7.2 0.7 copy-start
  7.2 308.8 %all-reduce.3.cloned.1.call-start = ((), (), s32[]{:S(2)}) async-start(), calls=%async_computation | async-start | bytes 4194304 | tf_op jit(solution)/shard_map/psum | solution.py:1195
  11.8 1.3 copy-start.6
  13.1 1.6 copy-start.20
  13.1 2.1 copy-start.27
  14.2 22.4 %collective-permute-start.1 = (bf16[4,256,512]{2,1,0:T(8,128)(2,1)}, bf16[4,256,512]{2,1,0:T(8,128)(2,1)}, u32[]{:S(2)}, u32[]{:S(2)}) collective-permute-start(bf16[4,256,512]{2,1,0:T(8,128)(2,1)} %constant_dynamic-slice_fusion.6), channel_id=1, source_target_pairs={{1,0},{0,1},{3,2},{2,3},{5,4},{4,5},{7,6},{6,7},{9,8},{8,9},{11,10... | collective-permute-start | bytes 3145736 | tf_op jit(solution)/shard_map/ppermute | solution.py:658
  14.6 20.2 %collective-permute-start.3 = (bf16[3,512,256]{2,1,0:T(8,128)(2,1)}, bf16[3,512,256]{2,1,0:T(8,128)(2,1)}, u32[]{:S(2)}, u32[]{:S(2)}) collective-permute-start(bf16[3,512,256]{2,1,0:T(8,128)(2,1)} %param.31), channel_id=1, source_target_pairs={{1,0},{0,1},{3,2},{2,3},{5,4},{4,5},{7,6},{6,7},{9,8},{8,9},{11,10... | collective-permute-start | bytes 2359304 | tf_op jit(solution)/shard_map/ppermute | solution.py:658
  14.7 12.3 %collective-permute-start.4 = (bf16[256,512]{1,0:T(8,128)(2,1)S(1)}, bf16[256,512]{1,0:T(8,128)(2,1)}, u32[]{:S(2)}, u32[]{:S(2)}) collective-permute-start(bf16[256,512]{1,0:T(8,128)(2,1)S(1)} %copy-done.20), channel_id=1, source_target_pairs={{1,0},{0,1},{3,2},{2,3},{5,4},{4,5},{7,6},{6,7},{9,8},{8,9},{11,10... | collective-permute-start | bytes 786440 | tf_op jit(solution)/shard_map/ppermute | solution.py:658
  15.2 14.2 %collective-permute-start.5 = (bf16[512,256]{1,0:T(8,128)(2,1)}, bf16[512,256]{1,0:T(8,128)(2,1)}, u32[]{:S(2)}, u32[]{:S(2)}) collective-permute-start(bf16[512,256]{1,0:T(8,128)(2,1)} %param.33), channel_id=1, source_target_pairs={{1,0},{0,1},{3,2},{2,3},{5,4},{4,5},{7,6},{6,7},{9,8},{8,9},{11,10... | collective-permute-start | bytes 786440 | tf_op jit(solution)/shard_map/ppermute | solution.py:658
  15.2 11.8 %collective-permute-start.8 = (bf16[4,256]{1,0:T(4,128)(2,1)S(1)}, bf16[4,256]{1,0:T(4,128)(2,1)S(1)}, u32[]{:S(2)}, u32[]{:S(2)}) collective-permute-start(bf16[4,256]{1,0:T(4,128)(2,1)S(1)} %copy-done.27), channel_id=1, source_target_pairs={{1,0},{0,1},{3,2},{2,3},{5,4},{4,5},{7,6},{6,7},{9,8},{8,9},{11,10... | collective-permute-start | bytes 6152 | tf_op jit(solution)/shard_map/ppermute | solution.py:658
  15.7 3.8 copy-start.25
  20.2 9.1 %copy-start.26 = (bf16[1024]{0:T(1024)(128)(2,1)S(1)}, bf16[1024]{0:T(1024)(128)(2,1)}, u32[]{:S(2)}) copy-start(bf16[1024]{0:T(1024)(128)(2,1)} %param.39) | copy-start | bytes 6148
  27.0 6.7 %collective-permute-start.6 = (bf16[2,512,256]{2,1,0:T(8,128)(2,1)}, bf16[2,512,256]{2,1,0:T(8,128)(2,1)}, u32[]{:S(2)}, u32[]{:S(2)}) collective-permute-start(bf16[2,512,256]{2,1,0:T(8,128)(2,1)} %param.34), channel_id=1, source_target_pairs={{1,0},{0,1},{3,2},{2,3},{5,4},{4,5},{7,6},{6,7},{9,8},{8,9},{11,10... | collective-permute-start | bytes 1572872 | tf_op jit(solution)/shard_map/ppermute | solution.py:658
  27.0 12.1 %collective-permute-start.2 = (bf16[4,256,512]{2,1,0:T(8,128)(2,1)}, bf16[4,256,512]{2,1,0:T(8,128)(2,1)}, u32[]{:S(2)}, u32[]{:S(2)}) collective-permute-start(bf16[4,256,512]{2,1,0:T(8,128)(2,1)} %constant_dynamic-slice_fusion.5), channel_id=1, source_target_pairs={{1,0},{0,1},{3,2},{2,3},{5,4},{4,5},{7,6},{6,7},{9,8},{8,9},{11,10... | collective-permute-start | bytes 3145736 | tf_op jit(solution)/shard_map/ppermute | solution.py:658
  29.3 7.2 %copy-start.21 = (bf16[1,1024]{1,0:T(2,128)(2,1)}, bf16[1,1024]{1,0:T(2,128)(2,1)S(1)}, u32[]{:S(2)}) copy-start(bf16[1,1024]{1,0:T(2,128)(2,1)S(1)} %broadcast_in_dim.45.refs_6_.refs_16_) | copy-start | bytes 6148
  29.4 3.2 collective-permute-start.7
  29.5 7.0 %copy-start.22 = (bf16[4,512]{1,0:T(4,128)(2,1)}, bf16[4,512]{1,0:T(4,128)(2,1)S(1)}, u32[]{:S(2)}) copy-start(bf16[4,512]{1,0:T(4,128)(2,1)S(1)} %constant_dynamic-update-slice_fusion.10.refs_11_) | copy-start | bytes 12292
  29.5 7.5 %copy-start.7 = (bf16[8,256,512]{2,1,0:T(8,128)(2,1)S(1)}, bf16[8,256,512]{2,1,0:T(8,128)(2,1)}, u32[]{:S(2)}) copy-start(bf16[8,256,512]{2,1,0:T(8,128)(2,1)} %copy-done.6) | copy-start | bytes 6291460
  30.6 8.5 %copy-start.9 = (bf16[512,512]{1,0:T(8,128)(2,1)}, bf16[512,512]{1,0:T(8,128)(2,1)S(1)}, u32[]{:S(2)}) copy-start(bf16[512,512]{1,0:T(8,128)(2,1)S(1)} %constant_dynamic-update-slice_fusion.2.refs_7_.refs_13_.refs_8_) | copy-start | bytes 1572868
  32.5 10.5 %collective-permute-start.9 = (bf16[4,256,512]{2,1,0:T(8,128)(2,1)}, bf16[4,256,512]{2,1,0:T(8,128)(2,1)S(1)}, u32[]{:S(2)}, u32[]{:S(2)}) collective-permute-start(bf16[4,256,512]{2,1,0:T(8,128)(2,1)} %constant_dynamic-slice_fusion.4), channel_id=1, source_target_pairs={{1,0},{0,1},{3,2},{2,3},{5,4},{4,5},{7,6},{6,7},{9,8},{8,9},{11,10... | collective-permute-start | bytes 3145736 | tf_op jit(solution)/shard_map/ppermute | solution.py:658
  33.7 54.7 %collective-permute-start.12 = (bf16[1,1024]{1,0:T(2,128)(2,1)S(1)}, bf16[1,1024]{1,0:T(2,128)(2,1)S(1)}, u32[]{:S(2)}, u32[]{:S(2)}) collective-permute-start(bf16[1,1024]{1,0:T(2,128)(2,1)S(1)} %broadcast_in_dim.45.refs_6_.refs_16_), channel_id=1, source_target_pairs={{1,0},{0,1},{3,2},{2,3},{5,4},{4,5},{7,6},{6,7},{9,8},{8,9},{11,10... | collective-permute-start | bytes 6152 | tf_op jit(solution)/shard_map/ppermute | solution.py:658
  34.8 4.3 %copy-start.8 = (bf16[2,512,512]{2,1,0:T(8,128)(2,1)}, bf16[2,512,512]{2,1,0:T(8,128)(2,1)S(1)}, u32[]{:S(2)}) copy-start(bf16[2,512,512]{2,1,0:T(8,128)(2,1)S(1)} %constant_dynamic-update-slice_fusion.6.refs_9_.refs_16_) | copy-start | bytes 3145732
  34.9 53.5 %collective-permute-start.10 = (bf16[512,1024]{1,0:T(8,128)(2,1)}, bf16[512,1024]{1,0:T(8,128)(2,1)}, u32[]{:S(2)}, u32[]{:S(2)}) collective-permute-start(bf16[512,1024]{1,0:T(8,128)(2,1)} %refs_12_.4), channel_id=1, source_target_pairs={{1,0},{0,1},{3,2},{2,3},{5,4},{4,5},{7,6},{6,7},{9,8},{8,9},{11,10... | collective-permute-start | bytes 3145736 | tf_op jit(solution)/shard_map/ppermute | solution.py:658
  36.6 2.6 copy-start.2
  36.6 2.6 copy-start.11
  36.6 51.8 %collective-permute-start.11 = (bf16[1024,512]{1,0:T(8,128)(2,1)}, bf16[1024,512]{1,0:T(8,128)(2,1)}, u32[]{:S(2)}, u32[]{:S(2)}) collective-permute-start(bf16[1024,512]{1,0:T(8,128)(2,1)} %refs_14_.4), channel_id=1, source_target_pairs={{1,0},{0,1},{3,2},{2,3},{5,4},{4,5},{7,6},{6,7},{9,8},{8,9},{11,10... | collective-permute-start | bytes 3145736 | tf_op jit(solution)/shard_map/ppermute | solution.py:658
  40.5 2.5 copy-start.12
  88.4 0.6 copy-start.24
  149.2 2.6 copy-start.16
  149.3 4.0 copy-start.5
  151.7 5.6 %collective-permute-start.14 = (bf16[512,1024]{1,0:T(8,128)(2,1)}, bf16[512,1024]{1,0:T(8,128)(2,1)}, u32[]{:S(2)}, u32[]{:S(2)}) collective-permute-start(bf16[512,1024]{1,0:T(8,128)(2,1)} %slice_bitcast_fusion), channel_id=1, source_target_pairs={{0,1},{1,0},{2,3},{3,2},{4,5},{5,4},{6,7},{7,6},{8,9},{9,8},{10,11... | collective-permute-start | bytes 3145736 | tf_op jit(solution)/shard_map/ppermute | solution.py:694
  153.0 7.0 %collective-permute-start.13 = (bf16[512,1024]{1,0:T(8,128)(2,1)}, bf16[512,1024]{1,0:T(8,128)(2,1)}, u32[]{:S(2)}, u32[]{:S(2)}) collective-permute-start(bf16[512,1024]{1,0:T(8,128)(2,1)} %slice_bitcast_fusion.1), channel_id=1, source_target_pairs={{0,1},{1,0},{2,3},{3,2},{4,5},{5,4},{6,7},{7,6},{8,9},{9,8},{10,11... | collective-permute-start | bytes 3145736 | tf_op jit(solution)/shard_map/ppermute | solution.py:694
  154.3 51.6 %collective-permute-start = (bf16[4,256,512]{2,1,0:T(8,128)(2,1)}, bf16[4,256,512]{2,1,0:T(8,128)(2,1)}, u32[]{:S(2)}, u32[]{:S(2)}) collective-permute-start(bf16[4,256,512]{2,1,0:T(8,128)(2,1)} %constant_dynamic-slice_fusion.8), channel_id=1, source_target_pairs={{1,0},{0,1},{3,2},{2,3},{5,4},{4,5},{7,6},{6,7},{9,8},{8,9},{11,10... | collective-permute-start | bytes 3145736 | tf_op jit(solution)/shard_map/ppermute | solution.py:658
  154.5 2.7 copy-start.18
  156.9 3.1 copy-start.17
  156.9 149.6 %collective-permute-start.16 = (bf16[4,256,512]{2,1,0:T(8,128)(2,1)}, bf16[4,256,512]{2,1,0:T(8,128)(2,1)S(1)}, u32[]{:S(2)}, u32[]{:S(2)}) collective-permute-start(bf16[4,256,512]{2,1,0:T(8,128)(2,1)} %constant_dynamic-slice_fusion.2), channel_id=1, source_target_pairs={{1,0},{0,1},{3,2},{2,3},{5,4},{4,5},{7,6},{6,7},{9,8},{8,9},{11,10... | collective-permute-start | bytes 3145736 | tf_op jit(solution)/shard_map/ppermute | solution.py:658
  205.9 102.6 %collective-permute-start.18 = (bf16[4,256,512]{2,1,0:T(8,128)(2,1)}, bf16[4,256,512]{2,1,0:T(8,128)(2,1)}, u32[]{:S(2)}, u32[]{:S(2)}) collective-permute-start(bf16[4,256,512]{2,1,0:T(8,128)(2,1)} %constant_dynamic-slice_fusion), channel_id=1, source_target_pairs={{1,0},{0,1},{3,2},{2,3},{5,4},{4,5},{7,6},{6,7},{9,8},{8,9},{11,10... | collective-permute-start | bytes 3145736 | tf_op jit(solution)/shard_map/ppermute | solution.py:658
  241.3 71.2 %collective-permute-start.17 = (bf16[4,256,512]{2,1,0:T(8,128)(2,1)}, bf16[4,256,512]{2,1,0:T(8,128)(2,1)}, u32[]{:S(2)}, u32[]{:S(2)}) collective-permute-start(bf16[4,256,512]{2,1,0:T(8,128)(2,1)} %constant_dynamic-slice_fusion.1), channel_id=1, source_target_pairs={{1,0},{0,1},{3,2},{2,3},{5,4},{4,5},{7,6},{6,7},{9,8},{8,9},{11,10... | collective-permute-start | bytes 3145736 | tf_op jit(solution)/shard_map/ppermute | solution.py:658
  243.1 63.4 %copy-start.13 = (bf16[4,512,512]{2,1,0:T(8,128)(2,1)S(1)}, bf16[4,512,512]{2,1,0:T(8,128)(2,1)}, u32[]{:S(2)}) copy-start(bf16[4,512,512]{2,1,0:T(8,128)(2,1)} %get-tuple-element.84) | copy-start | bytes 6291460
  307.0 2.3 copy-start.14
  311.0 2.3 copy-start.15
  312.5 3.5 copy-start.4
  316.0 1.6 copy-start.10
  317.0 82.9 %collective-permute-start.15 = (bf16[4,256,512]{2,1,0:T(8,128)(2,1)}, bf16[4,256,512]{2,1,0:T(8,128)(2,1)}, u32[]{:S(2)}, u32[]{:S(2)}) collective-permute-start(bf16[4,256,512]{2,1,0:T(8,128)(2,1)} %constant_dynamic-slice_fusion.3), channel_id=1, source_target_pairs={{1,0},{0,1},{3,2},{2,3},{5,4},{4,5},{7,6},{6,7},{9,8},{8,9},{11,10... | collective-permute-start | bytes 3145736 | tf_op jit(solution)/shard_map/ppermute | solution.py:658
  383.3 2.2 copy-start.3
  387.9 2.9 copy-start.23
  394.8 3.0 copy-start.19
  401.5 1.5 copy-start.1
Sparse Core Ops, SparseCore 0:
  162.8 129.7 all-reduce.2
